TPU v7x, 256 devices: a whole 4x4x8 slice. The times are simulated.
256 devices in a mesh: sp: 8 (over z), gx: 32 (over y, x, core).
Axes of the slice: x: 4, y: 4, z: 8, core: 2. Of those that a mesh axis runs over, the one named last changes fastest.
Arguments:
- tensor: float32 [64, 512, 6144], P('sp', 'gx'), may hold values from -32 to 32
- start_species: float32 [64, 16], replicated, may hold values from -4 to 4
- start_plane: float32 [512, 128], replicated, may hold values from -4 to 4
Outputs:
- core_block: float32 [6144, 16, 128], P(('sp', 'gx'))
- block_peaks: float32 [6144, 16], P(('sp', 'gx'))
All inputs are finite; a program needn't handle non-finite values.
Results may differ from a plain program's by a relative error of at most 0.0003.
Values sent between devices are 32-bit elements; how exact they have to be, the bound alone decides.
No kernel may reach another device: no remote copies, remote signals or barrier semaphores. Data moves between devices by JAX's collectives and lax.ppermute only.
A program may use at most 128 MiB of HBM per device.

v0:
```python
import jax
import jax.numpy as jnp
from jax import lax
from jax.experimental import pallas as pl
from jax.experimental.pallas import tpu as pltpu
from jax.sharding import PartitionSpec as P

SWEEPS = 4
HEIGHT = 2
F32 = jnp.float32
BF16 = jnp.bfloat16
BOTH = ("sp", "gx")
NN = (((1,), (0,)), ((), ()))
NT = (((1,), (1,)), ((), ()))
TN = (((0,), (0,)), ((), ()))
PAIR = [(d, d ^ 1) for d in range(32)]
PLANES = [[d + core for d in range(0, 32, 2)] for core in range(2)]


def grant(mebibytes):
    return pltpu.CompilerParams(vmem_limit_bytes=mebibytes * 1024 * 1024)


def exact_dot(a, b, dims=NN):
    return lax.dot_general(a, b, dims, precision=lax.Precision.HIGHEST, preferred_element_type=F32)


def bf16_dot(a, b, dims=NN):
    return lax.dot_general(a, b, dims, preferred_element_type=F32)


def split2(x):
    high = x.astype(BF16)
    return high, (x - high.astype(F32)).astype(BF16)


def split3(x):
    high = x.astype(BF16)
    rest = x - high.astype(F32)
    mid = rest.astype(BF16)
    return high, mid, (rest - mid.astype(F32)).astype(BF16)


def six(a, b, dims=NN):
    (ah, am, al), (bh, bm, bl) = a, b
    ka, kb = dims[0][0][0], dims[0][1][0]
    left = jnp.concatenate([ah, ah, am, ah, al, am], axis=ka)
    right = jnp.concatenate([bh, bm, bh, bl, bh, bm], axis=kb)
    return bf16_dot(left, right, dims)


def across(x, j):
    return jnp.broadcast_to(x[:, j : j + 1], (8, 128))


def full_row(x, i):
    return jnp.broadcast_to(x[i : i + 1, :], (8, 128))


def inverse_factor(panels, height=1, between=None):
    count = len(panels)
    sub = lax.broadcasted_iota(jnp.int32, (8, 128), 0)
    lane = lax.broadcasted_iota(jnp.int32, (8, 128), 1)
    state = list(panels)
    result = []
    for p in range(0, count, height):
        width = 8 * height
        own = (lane >= 8 * p) & (lane < 8 * p + width)
        cols = [[across(state[p + t], 8 * p + j) for t in range(height)] for j in range(width)]
        solved = [
            jnp.where(own, jnp.where(lane == sub + 8 * (p + t), 1.0, 0.0), state[p + t]) for t in range(height)
        ]
        rows = [jnp.where(lane < 8 * p + width, x, 0.0) for x in solved]
        root = [None] * height
        diag = full_row(cols[0][0], 0)
        for j in range(width):
            tj, ij = divmod(j, 8)
            recip = 1.0 / diag
            pivots = [full_row(cols[k][tj], ij) for k in range(j + 1, width)]
            if j + 1 < width:
                tn, i_n = divmod(j + 1, 8)
                diag = full_row(cols[j + 1][tn], i_n) - (full_row(cols[j][tn], i_n) * pivots[0]) * recip
            root[tj] = recip if ij == 0 else jnp.where(sub == ij, recip, root[tj])
            mult = []
            for t in range(height):
                m = cols[j][t] * recip
                mult.append(jnp.where(sub == ij, 0.0, m) if t == tj else m)
            for k in range(j + 1, width):
                cols[k] = [cols[k][t] - mult[t] * pivots[k - j - 1] for t in range(height)]
            pivot = full_row(solved[tj], ij)
            solved = [solved[t] - mult[t] * pivot for t in range(height)]
            pivot = full_row(rows[tj], ij)
            for t in range(tj, height):
                m = jnp.where(sub > ij, mult[t], 0.0) if t == tj else mult[t]
                rows[t] = rows[t] - m * pivot
        for t in range(height):
            result.append(rows[t] * jnp.sqrt(root[t]))
            solved[t] = solved[t] * root[t]
        near = min(p + 2 * height, count)
        for k in range(p + height, near):
            fresh = jnp.where(own, 0.0, state[k])
            for j in range(width):
                tj, ij = divmod(j, 8)
                fresh = fresh - across(state[k], 8 * p + j) * full_row(solved[tj], ij)
            state[k] = fresh
        if near < count:
            far = jnp.concatenate(state[near:], axis=0)
            ends = [jnp.zeros((8 * n, 128), F32) for n in (p, 16 - p - height)]
            weights = jnp.concatenate(([ends[0]] if p else []) + solved + [ends[1]], axis=0)
            change = six(split3(far), split3(weights))
            for k in range(near, count):
                at = 8 * (k - near)
                state[k] = jnp.where(own, 0.0, state[k]) - change[at : at + 8]
        if between is not None:
            between(p // height)
    return result


def subspace(gram, start, image_ref):
    split_gram = split3(gram)
    image_block = six(split_gram, split3(start))
    for sweep in range(SWEEPS):
        pieces = split3(image_block)
        inner = six(pieces, pieces, TN)
        step = 8 * HEIGHT

        def ahead(panel):
            rows = slice(4 * step * panel, 4 * step * (panel + 1))
            image_ref[rows, :] = six(tuple(g[rows] for g in split_gram), pieces)

        last = sweep + 1 == SWEEPS
        tiles = [inner[8 * p : 8 * p + 8] for p in range(16)]
        factor = split3(jnp.concatenate(inverse_factor(tiles, HEIGHT, None if last else ahead), axis=0))
        image_block = six(pieces if last else split3(image_ref[...]), factor, NT)
    return image_block


def subspace_narrow(gram, start):
    split_gram = split3(gram)
    image_block = six(split_gram, split3(start))
    blank = jnp.zeros((112, 128), F32)
    for sweep in range(SWEEPS):
        pieces = split3(image_block)
        inner = six(pieces, pieces, TN)
        ahead = pieces if sweep + 1 == SWEEPS else split3(six(split_gram, pieces))
        factor = inverse_factor([inner[0:8], inner[8:16]], 2)
        image_block = six(ahead, split3(jnp.concatenate(factor + [blank], axis=0)), NT)
    return image_block


def cells_first_kernel(x_ref, o_ref, tile_ref):
    for k in range(x_ref.shape[1] // 128):
        lanes = slice(128 * k, 128 * (k + 1))
        tile_ref[k] = x_ref[:, lanes]
        rows = jnp.concatenate([tile_ref[k, pl.ds(x, 8, stride=16), :] for x in range(16)], axis=0)
        o_ref[lanes, :] = rows.T


def cells_first(block):
    cells = block.shape[2]
    step = 768
    return pl.pallas_call(
        cells_first_kernel,
        out_shape=jax.ShapeDtypeStruct((cells, 128), F32),
        grid=(cells // step,),
        in_specs=[pl.BlockSpec((128, step), lambda i: (0, i))],
        out_specs=pl.BlockSpec((step, 128), lambda i: (i, 0)),
        scratch_shapes=[pltpu.VMEM((step // 128, 128, 128), F32)],
        compiler_params=grant(8),
    )(block.reshape(128, cells))


def species_gram_kernel(r_ref, o_ref, ht_ref, h_ref, l_ref):
    for s in range(8):
        high, low = split2(r_ref[s])
        ht_ref[128 * s : 128 * (s + 1), :] = r_ref[s].T.astype(BF16)
        h_ref[:, 128 * s : 128 * (s + 1)] = high
        l_ref[:, 128 * s : 128 * (s + 1)] = low
    lane = lax.broadcasted_iota(jnp.int32, (8, 256), 1) % 128
    rows = []
    for a in range(4):
        left = ht_ref[256 * a : 256 * (a + 1), :]
        parts = [[], []]
        for b in range(4):
            right = slice(256 * b, 256 * (b + 1))
            prod = bf16_dot(left, l_ref[:, right])
            if b >= a:
                main = bf16_dot(left, h_ref[:, right])
                prod = prod + (main if b > a else 0.5 * main)
            for half in range(2):
                acc = prod[128 * half : 128 * half + 8]
                for x in range(1, 16):
                    acc = jnp.where(lane // 8 == x, prod[128 * half + 8 * x : 128 * half + 8 * x + 8], acc)
                parts[half].append(acc)
        for half in range(2):
            rows.append(jnp.concatenate(parts[half], axis=1))
    wide = jnp.concatenate(rows, axis=0)
    fold = jnp.where(
        lax.broadcasted_iota(jnp.int32, (1024, 64), 0) // 128 * 8
        + lax.broadcasted_iota(jnp.int32, (1024, 64), 0) % 8
        == lax.broadcasted_iota(jnp.int32, (1024, 64), 1),
        1.0,
        0.0,
    ).astype(F32)
    half = exact_dot(wide, fold)
    gram = half + half.T
    o_ref[...] = jnp.concatenate([gram[0:32], gram[32:64]], axis=1)


def species_gram(received):
    return pl.pallas_call(
        species_gram_kernel,
        out_shape=jax.ShapeDtypeStruct((32, 128), F32),
        scratch_shapes=[
            pltpu.VMEM((1024, 768), BF16),
            pltpu.VMEM((768, 1024), BF16),
            pltpu.VMEM((768, 1024), BF16),
        ],
        compiler_params=grant(16),
    )(received)


def plane_gram_kernel(core_ref, r_ref, g_ref, start_ref, turned_ref, mine_ref, other_ref, wh_ref, wl_ref, red_ref):
    folded = jnp.sum(g_ref[...], axis=0)
    gram = jnp.concatenate([folded[:, 0:64], folded[:, 64:128]], axis=0)
    start = jnp.concatenate([start_ref[...], jnp.zeros((64, 112), F32)], axis=1)
    basis = subspace_narrow(gram, start)[:, 0:16]
    widen = jnp.where(
        lax.broadcasted_iota(jnp.int32, (16, 256), 1) // 16 == lax.broadcasted_iota(jnp.int32, (16, 256), 0), 1.0, 0.0
    ).astype(F32)
    wide = exact_dot(basis, widen)
    keep = (
        lax.broadcasted_iota(jnp.int32, (128, 256), 0) // 8 == lax.broadcasted_iota(jnp.int32, (128, 256), 1) % 16
    )
    for s in range(8):
        weights = jnp.where(keep, jnp.concatenate([wide[8 * s : 8 * s + 8]] * 16, axis=0), 0.0)
        high, low = split2(weights)
        wh_ref[128 * s : 128 * (s + 1), :] = high
        wl_ref[128 * s : 128 * (s + 1), :] = low
    total = None
    for s in range(8):
        high, low = split2(r_ref[s])
        rows = slice(128 * s, 128 * (s + 1))
        term = bf16_dot(high, wh_ref[rows]) + bf16_dot(high, wl_ref[rows]) + bf16_dot(low, wh_ref[rows])
        total = term if s == 0 else total + term
    red_ref[...] = total
    lane = lax.broadcasted_iota(jnp.int32, (16, 128), 1)
    blank = jnp.zeros((8, 256), F32)
    for a in range(8):
        rows = []
        for b in range(4):
            g = 4 * a + b
            rows += [red_ref[24 * g : 24 * g + 24, :], blank]
        turned = jnp.concatenate(rows, axis=0).T
        shifted = [turned] + [pltpu.roll(turned, 32 * k, 1) for k in range(1, 4)]
        for b in range(4):
            g = 4 * a + b
            for quad in range(4):
                block = None
                for k in range(4):
                    r = 4 * quad + k
                    piece = shifted[(k - b) % 4][16 * r : 16 * r + 16, :]
                    block = piece if k == 0 else jnp.where(lane // 32 == k, piece, block)
                turned_ref[16 * g : 16 * g + 16, 128 * quad : 128 * (quad + 1)] = block
    high, low = split2(turned_ref[...])
    left = jnp.concatenate([high, high, low], axis=1)
    right = jnp.concatenate([high, low, high], axis=1)
    blocks = []
    for i in range(4):
        for j in range(i, 4):
            blocks.append(bf16_dot(left[128 * i : 128 * (i + 1)], right[128 * j : 128 * (j + 1)], NT))
    first = core_ref[0] == 0
    for n in range(5):
        rows = slice(128 * n, 128 * (n + 1))
        mine_ref[rows, :] = jnp.where(first, blocks[n], blocks[n + 5])
        other_ref[rows, :] = jnp.where(first, blocks[n + 5], blocks[n])


def plane_gram(core, received, grams, start_species):
    half = jax.ShapeDtypeStruct((640, 128), F32)
    whole = pl.BlockSpec(memory_space=pltpu.VMEM)
    return pl.pallas_call(
        plane_gram_kernel,
        out_shape=(jax.ShapeDtypeStruct((512, 512), F32), half, half),
        in_specs=[pl.BlockSpec(memory_space=pltpu.SMEM), whole, whole, whole],
        scratch_shapes=[pltpu.VMEM((1024, 256), BF16), pltpu.VMEM((1024, 256), BF16), pltpu.VMEM((768, 256), F32)],
        compiler_params=grant(20),
    )(core, received, grams, start_species)


def core_kernel(core_ref, mine_ref, other_ref, turned_ref, start_ref, out_ref, peaks_ref, image_ref):
    first = core_ref[0] == 0
    blocks = {}
    n = 0
    for i in range(4):
        for j in range(i, 4):
            rows = slice(128 * (n % 5), 128 * (n % 5 + 1))
            mine, other = mine_ref[rows, :], other_ref[rows, :]
            blocks[i, j] = jnp.where(first, mine, other) if n < 5 else jnp.where(first, other, mine)
            if i != j:
                blocks[j, i] = blocks[i, j].T
            n += 1
    gram = jnp.concatenate(
        [jnp.concatenate([blocks[i, j] for j in range(4)], axis=1) for i in range(4)], axis=0
    )
    basis = subspace(gram, start_ref[...], image_ref)
    th, tl = split2(turned_ref[...].T)
    bh, bl = split2(basis)
    core = bf16_dot(th, bh) + bf16_dot(th, bl) + bf16_dot(tl, bh)
    for r in range(16):
        out_ref[pl.ds(r, 24, stride=16), :] = core[32 * r : 32 * r + 24, :]
    peaks = jnp.max(jnp.abs(core).reshape(16, 32, 128), axis=2)
    peaks_ref[...] = peaks.T[0:24]


def core_of(core, mine, other, turned, start_plane):
    whole = pl.BlockSpec(memory_space=pltpu.VMEM)
    return pl.pallas_call(
        core_kernel,
        out_shape=(jax.ShapeDtypeStruct((384, 128), F32), jax.ShapeDtypeStruct((24, 16), F32)),
        in_specs=[pl.BlockSpec(memory_space=pltpu.SMEM), whole, whole, whole, whole],
        scratch_shapes=[pltpu.VMEM((512, 128), F32)],
        compiler_params=grant(20),
    )(core, mine, other, turned, start_plane)


def over_plane(x):
    return lax.all_to_all(x, "gx", 0, 0, tiled=True, axis_index_groups=PLANES)


def copies(x, count):
    return jnp.broadcast_to(x[None], (count,) + x.shape)


def per_device(tensor, start_species, start_plane):
    core = (lax.axis_index("gx") % 2).astype(jnp.int32).reshape(1)
    sent = cells_first(tensor).reshape(256, 24, 128)
    received = lax.all_to_all(sent, BOTH, 0, 0, tiled=True).reshape(8, 768, 128)
    grams = species_gram(received)
    grams = grams + lax.ppermute(grams, "gx", PAIR)
    grams = jnp.sum(over_plane(copies(grams, 16)), axis=0)
    grams = lax.all_to_all(copies(grams, 8), "sp", 0, 0, tiled=True)
    turned, mine, other = plane_gram(core, received, grams, start_species)
    mine = mine + lax.ppermute(other, "gx", PAIR)
    share = jnp.sum(over_plane(mine.reshape(16, 40, 128)), axis=0)
    share = jnp.sum(lax.all_to_all(copies(share, 8), "sp", 0, 0, tiled=True), axis=0)
    mine = over_plane(copies(share, 16)).reshape(640, 128)
    other = lax.ppermute(mine, "gx", PAIR)
    core_block, block_peaks = core_of(core, mine, other, turned, start_plane)
    return core_block.reshape(24, 16, 128), block_peaks


def solution(mesh):
    placed = (P("sp", "gx", None), P(), P())
    return jax.shard_map(
        per_device,
        mesh=mesh,
        in_specs=placed,
        out_specs=(P(BOTH, None, None), P(BOTH, None)),
        check_vma=False,
    )
```

profile of v0, /device:TPU:1, one launch (start us, length us, event | category | flops | bytes accessed | tf_op | source)
XLA Modules:
  0.0 196.7 jit_solution(6332204591617671032)
XLA Ops:
  0.6 0.0 copy-start
  0.6 1.9 copy-done
  2.5 2.0 shard_map.50
  4.5 91.1 %all_to_all.30 = f32[256,24,128]{2,1,0:T(8,128)S(1)} all-to-all(f32[256,24,128]{2,1,0:T(8,128)S(1)} %bitcast.9), channel_id=1, replica_groups=mesh['sp'=8,'gx'=32] {'sp','gx'}, dimensions={0} | all-to-all | bytes 6291456 | tf_op jit(solution)/shard_map/all_to_all | solution.py:338
  95.6 0.0 copy-start.5
  95.6 3.5 %shard_map.51 = f32[32,128]{1,0:T(8,128)S(1)} custom-call(f32[8,768,128]{2,1,0:T(8,128)S(1)} %bitcast.7), custom_call_target="tpu_custom_call" | custom-call | tf_op jit(solution)/shard_map/pallas_call | solution.py:211
  99.1 0.9 collective-permute-start
  100.0 0.8 collective-permute-done
  100.8 12.0 %all_to_all.31 = f32[16,32,128]{2,1,0:T(8,128)S(1)} all-to-all(f32[16,32,128]{2,1,0:T(8,128)S(1)} %broadcast_in_dim.8), channel_id=1, replica_groups={{0,2,4,6,8,10,12,14,16,18,20,22,24,26,28,30},{1,3,5,7,9,11,13,15,17,19,..., dimensions={0} | all-to-all | bytes 524288 | tf_op jit(solution)/shard_map/all_to_all | solution.py:328
  112.8 0.7 broadcast_in_dim.9
  113.5 3.4 %all-to-all-start.2 = ((f32[8,32,128]{2,1,0:T(8,128)}), f32[8,32,128]{2,1,0:T(8,128)S(1)}, u32[]{:S(2)}, u32[]{:S(2)}) async-start(f32[8,32,128]{2,1,0:T(8,128)} %broadcast_in_dim.9), calls=%async_computation.2 | async-start | bytes 262144 | tf_op jit(solution)/shard_map/all_to_all | solution.py:342
  116.9 0.0 copy-done.5
  116.9 0.7 copy.7.start_ref
  117.6 7.2 %all-to-all-done.2.g_ref = f32[8,32,128]{2,1,0:T(8,128)S(1)} async-done(((f32[8,32,128]{2,1,0:T(8,128)}), f32[8,32,128]{2,1,0:T(8,128)S(1)}, u32[]{:S(2)}, u32[]{:S(2)}) %all-to-all-start.2) | async-done | bytes 131104 | tf_op jit(solution)/shard_map/all_to_all | solution.py:342
  124.7 0.0 copy-start.4
  124.7 0.8 copy-done.4
  125.5 0.0 copy-start.3
  125.5 9.5 %shard_map.52 = (f32[512,512]{1,0:T(8,128)S(1)}, f32[640,128]{1,0:T(8,128)S(1)}, f32[640,128]{1,0:T(8,128)S(1)}) custom-call(s32[1]{0:T(128)} %bitcast.core_ref, f32[8,768,128]{2,1,0:T(8,128)S(1)} %bitcast.8, f32[8,32,128]{2,1,0:T(8,128)S(1)} %all-to-all-done.2.g_ref, f32[64,16]{1,0:T(8,128)S(1)} %copy-done.4), custom_call_target="tpu_custom_call" | custom-call | tf_op jit(solution)/shard_map/pallas_call | solution.py:282
  135.0 0.0 copy-start.1
  135.0 1.0 copy-done.1
  136.0 0.0 copy-start.2
  136.0 2.6 %collective-permute-start.1 = (f32[640,128]{1,0:T(8,128)S(1)}, f32[640,128]{1,0:T(8,128)S(1)}, u32[]{:S(2)}, u32[]{:S(2)}) collective-permute-start(f32[640,128]{1,0:T(8,128)S(1)} %get-tuple-element.8), channel_id=1, source_target_pairs={{0,1},{1,0},{2,3},{3,2},{4,5},{5,4},{6,7},{7,6},{8,9},{9,8},{10,11... | collective-permute-start | bytes 983048 | tf_op jit(solution)/shard_map/ppermute | solution.py:344
  138.6 1.3 collective-permute-done.1
  139.9 11.4 %all_to_all.32 = f32[16,40,128]{2,1,0:T(8,128)S(1)} all-to-all(f32[16,40,128]{2,1,0:T(8,128)S(1)} %bitcast.13), channel_id=1, replica_groups={{0,2,4,6,8,10,12,14,16,18,20,22,24,26,28,30},{1,3,5,7,9,11,13,15,17,19,..., dimensions={0} | all-to-all | bytes 655360 | tf_op jit(solution)/shard_map/all_to_all | solution.py:328
  151.4 10.8 %all_to_all.33 = f32[8,40,128]{2,1,0:T(8,128)S(1)} all-to-all(f32[8,40,128]{2,1,0:T(8,128)S(1)} %broadcast_in_dim.10), channel_id=1, replica_groups=mesh['sp'=8,'gx'=32] {'sp'}, dimensions={0} | all-to-all | bytes 327680 | tf_op jit(solution)/shard_map/all_to_all | solution.py:346
  162.2 10.6 %all_to_all.34 = f32[16,40,128]{2,1,0:T(8,128)S(1)} all-to-all(f32[16,40,128]{2,1,0:T(8,128)S(1)} %broadcast_in_dim.11), channel_id=1, replica_groups={{0,2,4,6,8,10,12,14,16,18,20,22,24,26,28,30},{1,3,5,7,9,11,13,15,17,19,..., dimensions={0} | all-to-all | bytes 655360 | tf_op jit(solution)/shard_map/all_to_all | solution.py:328
  172.8 3.9 %collective-permute-start.2 = (f32[640,128]{1,0:T(8,128)S(1)}, f32[640,128]{1,0:T(8,128)S(1)}, u32[]{:S(2)}, u32[]{:S(2)}) collective-permute-start(f32[640,128]{1,0:T(8,128)S(1)} %bitcast.11), channel_id=1, source_target_pairs={{0,1},{1,0},{2,3},{3,2},{4,5},{5,4},{6,7},{7,6},{8,9},{9,8},{10,11... | collective-permute-start | bytes 983048 | tf_op jit(solution)/shard_map/ppermute | solution.py:348
  176.7 1.3 collective-permute-done.2.other_ref
  178.0 0.0 copy-done.3
  178.0 0.0 copy-done.2
  178.0 18.1 %shard_map.53 = (f32[384,128]{1,0:T(8,128)}, f32[24,16]{1,0:T(8,128)S(1)}) custom-call(s32[1]{0:T(128)} %bitcast.core_ref, f32[640,128]{1,0:T(8,128)S(1)} %bitcast.12, f32[640,128]{1,0:T(8,128)S(1)} %collective-permute-done.2.other_ref, f32[512,512]{1,0:T(8,128)S(1)} %copy-done.2, f32[512,128]{1,0:T(8,128)S(1)} %copy-done.3), custom_call_target="tpu_custom_call" | custom-call | tf_op jit(solution)/shard_map/pallas_call | solution.py:318
  196.1 0.7 copy.8
  (8 shorter events, 0.2 us)
Async XLA Ops:
  0.6 1.9 copy-start
  95.6 21.3 %copy-start.5 = (f32[64,16]{0,1:T(8,128)S(1)}, f32[64,16]{0,1:T(8,128)}, u32[]{:S(2)}) copy-start(f32[64,16]{0,1:T(8,128)} %param.4) | copy-start | bytes 12292
  99.1 1.7 collective-permute-start
  113.5 11.2 %all-to-all-start.2 = ((f32[8,32,128]{2,1,0:T(8,128)}), f32[8,32,128]{2,1,0:T(8,128)S(1)}, u32[]{:S(2)}, u32[]{:S(2)}) async-start(f32[8,32,128]{2,1,0:T(8,128)} %broadcast_in_dim.9), calls=%async_computation.2 | async-start | bytes 262144 | tf_op jit(solution)/shard_map/all_to_all | solution.py:342
  124.7 0.8 copy-start.4
  125.5 52.5 %copy-start.3 = (f32[512,128]{1,0:T(8,128)S(1)}, f32[512,128]{1,0:T(8,128)}, u32[]{:S(2)}) copy-start(f32[512,128]{1,0:T(8,128)} %start_ref.2) | copy-start | bytes 786436
  135.0 1.0 copy-start.1
  136.0 42.0 %copy-start.2 = (f32[512,512]{1,0:T(8,128)S(1)}, f32[512,512]{1,0:T(8,128)}, u32[]{:S(2)}) copy-start(f32[512,512]{1,0:T(8,128)} %copy-done.1) | copy-start | bytes 3145732
  136.0 3.9 %collective-permute-start.1 = (f32[640,128]{1,0:T(8,128)S(1)}, f32[640,128]{1,0:T(8,128)S(1)}, u32[]{:S(2)}, u32[]{:S(2)}) collective-permute-start(f32[640,128]{1,0:T(8,128)S(1)} %get-tuple-element.8), channel_id=1, source_target_pairs={{0,1},{1,0},{2,3},{3,2},{4,5},{5,4},{6,7},{7,6},{8,9},{9,8},{10,11... | collective-permute-start | bytes 983048 | tf_op jit(solution)/shard_map/ppermute | solution.py:344
  172.8 5.2 %collective-permute-start.2 = (f32[640,128]{1,0:T(8,128)S(1)}, f32[640,128]{1,0:T(8,128)S(1)}, u32[]{:S(2)}, u32[]{:S(2)}) collective-permute-start(f32[640,128]{1,0:T(8,128)S(1)} %bitcast.11), channel_id=1, source_target_pairs={{0,1},{1,0},{2,3},{3,2},{4,5},{5,4},{6,7},{7,6},{8,9},{9,8},{10,11... | collective-permute-start | bytes 983048 | tf_op jit(solution)/shard_map/ppermute | solution.py:348
where the time goes:
time: 197 us
  blocking collectives  136 us (69%)
  Pallas kernels  33.1 us (17%)
  starting transfers between devices  10.8 us (5%)
  waiting for transfers between devices  10.5 us (5%)
  local copies, waits for them, and re-layouts  5.69 us (3%)
    all_to_all x1, blocking collectives, per_device(): received = lax.all_to_all(sent, BOTH, 0, 0, tiled=True).reshape(8, 768, 128)  91.1 us
    all_to_all x3, blocking collectives, over_plane(): return lax.all_to_all(x, 'gx', 0, 0, tiled=True, axis_index_groups=PLANES)  34 us
    pallas_call x1, Pallas kernels, core_of(): pl.pallas_call(core_kernel, out_shape=(jax.ShapeDtypeStruct((384, 128), F...  18.1 us
    all_to_all x1, blocking collectives, per_device(): lax.all_to_all(copies(share, 8), 'sp', 0, 0, tiled=True)  10.8 us
    pallas_call x1, Pallas kernels, plane_gram(): pl.pallas_call(plane_gram_kernel, out_shape=(jax.ShapeDtypeStruct((512, 5...  9.51 us
    all_to_all x1, waiting for transfers between devices, per_device(): grams = lax.all_to_all(copies(grams, 8), 'sp', 0, 0, tiled=True)  7.16 us
    unnamed x14, local copies, waits for them, and re-layouts  4.97 us
  transfers between devices with their start and end apart: 4, of which 4 were waited for; matrix products, arithmetic and copies ran while one was open for 0% of the time, Pallas kernels for 0%

commit v1 on v0

--- a/solution.py
+++ b/solution.py
@@ -7,6 +7,8 @@
 
 SWEEPS = 4
 HEIGHT = 2
+CHUNKS = 4
+SPARE = 32768
 F32 = jnp.float32
 BF16 = jnp.bfloat16
 BOTH = ("sp", "gx")
@@ -43,10 +45,22 @@
 
 def six(a, b, dims=NN):
     (ah, am, al), (bh, bm, bl) = a, b
-    ka, kb = dims[0][0][0], dims[0][1][0]
-    left = jnp.concatenate([ah, ah, am, ah, al, am], axis=ka)
-    right = jnp.concatenate([bh, bm, bh, bl, bh, bm], axis=kb)
-    return bf16_dot(left, right, dims)
+    (ka,), (kb,) = dims[0]
+    n = bh.shape[1 - kb]
+    left = jnp.concatenate([ah, am], axis=ka)
+    right = jnp.concatenate([jnp.concatenate([x, x], axis=kb) for x in (bh, bm)], axis=1 - kb)
+    main = bf16_dot(left, right, dims)
+    rest = bf16_dot(jnp.concatenate([al, ah], axis=ka), jnp.concatenate([bh, bl], axis=kb), dims)
+    return main[:, :n] + (main[:, n:] + rest)
+
+
+def six_gram(a):
+    high, mid, low = a
+    left = jnp.concatenate([high, mid, low], axis=1)
+    got = bf16_dot(left, jnp.concatenate([high, mid], axis=1), TN)
+    small = got[256:384, 0:128]
+    cross = got[0:128, 128:256] + got[128:256, 0:128]
+    return got[0:128, 0:128] + (cross + (got[128:256, 128:256] + (small + small.T)))
 
 
 def across(x, j):
@@ -119,54 +133,76 @@
 def subspace(gram, start, image_ref):
     split_gram = split3(gram)
     image_block = six(split_gram, split3(start))
+    chunk = gram.shape[0] // CHUNKS
     for sweep in range(SWEEPS):
         pieces = split3(image_block)
-        inner = six(pieces, pieces, TN)
-        step = 8 * HEIGHT
+        inner = six_gram(pieces)
+        last = sweep + 1 == SWEEPS
 
         def ahead(panel):
-            rows = slice(4 * step * panel, 4 * step * (panel + 1))
-            image_ref[rows, :] = six(tuple(g[rows] for g in split_gram), pieces)
-
-        last = sweep + 1 == SWEEPS
+            if panel < CHUNKS and not last:
+                rows = slice(chunk * panel, chunk * (panel + 1))
+                image_ref[rows, :] = six(tuple(g[rows] for g in split_gram), pieces)
+
         tiles = [inner[8 * p : 8 * p + 8] for p in range(16)]
-        factor = split3(jnp.concatenate(inverse_factor(tiles, HEIGHT, None if last else ahead), axis=0))
+        factor = split3(jnp.concatenate(inverse_factor(tiles, HEIGHT, ahead), axis=0))
         image_block = six(pieces if last else split3(image_ref[...]), factor, NT)
     return image_block
 
 
-def subspace_narrow(gram, start):
+def subspace_narrow(gram, start, between):
     split_gram = split3(gram)
     image_block = six(split_gram, split3(start))
     blank = jnp.zeros((112, 128), F32)
     for sweep in range(SWEEPS):
         pieces = split3(image_block)
-        inner = six(pieces, pieces, TN)
+        inner = six_gram(pieces)
         ahead = pieces if sweep + 1 == SWEEPS else split3(six(split_gram, pieces))
+        between(sweep)
         factor = inverse_factor([inner[0:8], inner[8:16]], 2)
         image_block = six(ahead, split3(jnp.concatenate(factor + [blank], axis=0)), NT)
     return image_block
 
 
-def cells_first_kernel(x_ref, o_ref, tile_ref):
-    for k in range(x_ref.shape[1] // 128):
-        lanes = slice(128 * k, 128 * (k + 1))
-        tile_ref[k] = x_ref[:, lanes]
-        rows = jnp.concatenate([tile_ref[k, pl.ds(x, 8, stride=16), :] for x in range(16)], axis=0)
-        o_ref[lanes, :] = rows.T
+STEPS = 8
+
+
+def cells_first_kernel(x_ref, o_ref, tile_ref, turned_ref, in_sems, out_sems):
+    step = o_ref.shape[0] // STEPS
+    loads = [
+        pltpu.make_async_copy(x_ref.at[:, pl.ds(step * k, step)], tile_ref.at[k], in_sems.at[k]) for k in range(STEPS)
+    ]
+    stores = [
+        pltpu.make_async_copy(turned_ref.at[k], o_ref.at[pl.ds(step * k, step)], out_sems.at[k]) for k in range(STEPS)
+    ]
+    for load in loads:
+        load.start()
+    for k in range(STEPS):
+        loads[k].wait()
+        for n in range(step // 128):
+            tile = tile_ref[k, :, 128 * n : 128 * (n + 1)].reshape(8, 16, 128)
+            rows = jnp.concatenate([tile[:, x, :] for x in range(16)], axis=0)
+            turned_ref[k, 128 * n : 128 * (n + 1), :] = rows.T
+        stores[k].start()
+    for store in stores:
+        store.wait()
 
 
 def cells_first(block):
     cells = block.shape[2]
-    step = 768
+    step = cells // STEPS
     return pl.pallas_call(
         cells_first_kernel,
         out_shape=jax.ShapeDtypeStruct((cells, 128), F32),
-        grid=(cells // step,),
-        in_specs=[pl.BlockSpec((128, step), lambda i: (0, i))],
-        out_specs=pl.BlockSpec((step, 128), lambda i: (i, 0)),
-        scratch_shapes=[pltpu.VMEM((step // 128, 128, 128), F32)],
-        compiler_params=grant(8),
+        in_specs=[pl.BlockSpec(memory_space=pltpu.HBM)],
+        out_specs=pl.BlockSpec(memory_space=pltpu.HBM),
+        scratch_shapes=[
+            pltpu.VMEM((STEPS, 128, step), F32),
+            pltpu.VMEM((STEPS, step, 128), F32),
+            pltpu.SemaphoreType.DMA((STEPS,)),
+            pltpu.SemaphoreType.DMA((STEPS,)),
+        ],
+        compiler_params=grant(56),
     )(block.reshape(128, cells))
 
 
@@ -220,15 +256,23 @@
     )(received)
 
 
-def plane_gram_kernel(core_ref, r_ref, g_ref, start_ref, turned_ref, mine_ref, other_ref, wh_ref, wl_ref, red_ref):
+def plane_gram_kernel(
+    core_ref, r_ref, g_ref, start_ref, out_ref, mine_ref, other_ref, wh_ref, wl_ref, h_ref, l_ref, red_ref, turned_ref, sem
+):
+    def between(sweep):
+        for s in (2 * sweep, 2 * sweep + 1):
+            lanes = slice(128 * s, 128 * (s + 1))
+            h_ref[:, lanes], l_ref[:, lanes] = split2(r_ref[s])
+
     folded = jnp.sum(g_ref[...], axis=0)
     gram = jnp.concatenate([folded[:, 0:64], folded[:, 64:128]], axis=0)
-    start = jnp.concatenate([start_ref[...], jnp.zeros((64, 112), F32)], axis=1)
-    basis = subspace_narrow(gram, start)[:, 0:16]
+    start = jnp.concatenate([start_ref[...], jnp.zeros((112, 64), F32)], axis=0).T
+    basis = subspace_narrow(gram, start, between)[:, 0:16]
     widen = jnp.where(
         lax.broadcasted_iota(jnp.int32, (16, 256), 1) // 16 == lax.broadcasted_iota(jnp.int32, (16, 256), 0), 1.0, 0.0
-    ).astype(F32)
-    wide = exact_dot(basis, widen)
+    ).astype(BF16)
+    high, mid, low = split3(basis)
+    wide = bf16_dot(jnp.concatenate([high, mid, low], axis=1), jnp.concatenate([widen] * 3, axis=0))
     keep = (
         lax.broadcasted_iota(jnp.int32, (128, 256), 0) // 8 == lax.broadcasted_iota(jnp.int32, (128, 256), 1) % 16
     )
@@ -237,12 +281,8 @@
         high, low = split2(weights)
         wh_ref[128 * s : 128 * (s + 1), :] = high
         wl_ref[128 * s : 128 * (s + 1), :] = low
-    total = None
-    for s in range(8):
-        high, low = split2(r_ref[s])
-        rows = slice(128 * s, 128 * (s + 1))
-        term = bf16_dot(high, wh_ref[rows]) + bf16_dot(high, wl_ref[rows]) + bf16_dot(low, wh_ref[rows])
-        total = term if s == 0 else total + term
+    wh = wh_ref[...]
+    total = bf16_dot(h_ref[...], wh) + (bf16_dot(h_ref[...], wl_ref[...]) + bf16_dot(l_ref[...], wh))
     red_ref[...] = total
     lane = lax.broadcasted_iota(jnp.int32, (16, 128), 1)
     blank = jnp.zeros((8, 256), F32)
@@ -262,6 +302,8 @@
                     piece = shifted[(k - b) % 4][16 * r : 16 * r + 16, :]
                     block = piece if k == 0 else jnp.where(lane // 32 == k, piece, block)
                 turned_ref[16 * g : 16 * g + 16, 128 * quad : 128 * (quad + 1)] = block
+    copy = pltpu.make_async_copy(turned_ref, out_ref.at[pl.ds(0, 512)], sem)
+    copy.start()
     high, low = split2(turned_ref[...])
     left = jnp.concatenate([high, high, low], axis=1)
     right = jnp.concatenate([high, low, high], axis=1)
@@ -274,6 +316,7 @@
         rows = slice(128 * n, 128 * (n + 1))
         mine_ref[rows, :] = jnp.where(first, blocks[n], blocks[n + 5])
         other_ref[rows, :] = jnp.where(first, blocks[n + 5], blocks[n])
+    copy.wait()
 
 
 def plane_gram(core, received, grams, start_species):
@@ -281,14 +324,27 @@
     whole = pl.BlockSpec(memory_space=pltpu.VMEM)
     return pl.pallas_call(
         plane_gram_kernel,
-        out_shape=(jax.ShapeDtypeStruct((512, 512), F32), half, half),
+        out_shape=(jax.ShapeDtypeStruct((SPARE, 512), F32), half, half),
         in_specs=[pl.BlockSpec(memory_space=pltpu.SMEM), whole, whole, whole],
-        scratch_shapes=[pltpu.VMEM((1024, 256), BF16), pltpu.VMEM((1024, 256), BF16), pltpu.VMEM((768, 256), F32)],
+        out_specs=(pl.BlockSpec(memory_space=pltpu.HBM), whole, whole),
+        scratch_shapes=[
+            pltpu.VMEM((1024, 256), BF16),
+            pltpu.VMEM((1024, 256), BF16),
+            pltpu.VMEM((768, 1024), BF16),
+            pltpu.VMEM((768, 1024), BF16),
+            pltpu.VMEM((768, 256), F32),
+            pltpu.VMEM((512, 512), F32),
+            pltpu.SemaphoreType.DMA,
+        ],
         compiler_params=grant(20),
-    )(core, received, grams, start_species)
-
-
-def core_kernel(core_ref, mine_ref, other_ref, turned_ref, start_ref, out_ref, peaks_ref, image_ref):
+    )(core, received, grams, start_species.T)
+
+
+def core_kernel(
+    core_ref, mine_ref, other_ref, turned_hbm, start_ref, out_ref, peaks_ref, image_ref, turned_ref, sem
+):
+    copy = pltpu.make_async_copy(turned_hbm.at[pl.ds(0, 512)], turned_ref, sem)
+    copy.start()
     first = core_ref[0] == 0
     blocks = {}
     n = 0
@@ -304,22 +360,23 @@
         [jnp.concatenate([blocks[i, j] for j in range(4)], axis=1) for i in range(4)], axis=0
     )
     basis = subspace(gram, start_ref[...], image_ref)
+    copy.wait()
     th, tl = split2(turned_ref[...].T)
     bh, bl = split2(basis)
     core = bf16_dot(th, bh) + bf16_dot(th, bl) + bf16_dot(tl, bh)
     for r in range(16):
         out_ref[pl.ds(r, 24, stride=16), :] = core[32 * r : 32 * r + 24, :]
     peaks = jnp.max(jnp.abs(core).reshape(16, 32, 128), axis=2)
-    peaks_ref[...] = peaks.T[0:24]
+    peaks_ref[...] = peaks[:, 0:24]
 
 
 def core_of(core, mine, other, turned, start_plane):
     whole = pl.BlockSpec(memory_space=pltpu.VMEM)
     return pl.pallas_call(
         core_kernel,
-        out_shape=(jax.ShapeDtypeStruct((384, 128), F32), jax.ShapeDtypeStruct((24, 16), F32)),
-        in_specs=[pl.BlockSpec(memory_space=pltpu.SMEM), whole, whole, whole, whole],
-        scratch_shapes=[pltpu.VMEM((512, 128), F32)],
+        out_shape=(jax.ShapeDtypeStruct((384, 128), F32), jax.ShapeDtypeStruct((16, 24), F32)),
+        in_specs=[pl.BlockSpec(memory_space=pltpu.SMEM), whole, whole, pl.BlockSpec(memory_space=pltpu.HBM), whole],
+        scratch_shapes=[pltpu.VMEM((512, 128), F32), pltpu.VMEM((512, 512), F32), pltpu.SemaphoreType.DMA],
         compiler_params=grant(20),
     )(core, mine, other, turned, start_plane)
 
@@ -336,7 +393,7 @@
     core = (lax.axis_index("gx") % 2).astype(jnp.int32).reshape(1)
     sent = cells_first(tensor).reshape(256, 24, 128)
     received = lax.all_to_all(sent, BOTH, 0, 0, tiled=True).reshape(8, 768, 128)
-    grams = species_gram(received)
+    grams, core = lax.optimization_barrier((species_gram(received), core))
     grams = grams + lax.ppermute(grams, "gx", PAIR)
     grams = jnp.sum(over_plane(copies(grams, 16)), axis=0)
     grams = lax.all_to_all(copies(grams, 8), "sp", 0, 0, tiled=True)
@@ -347,7 +404,7 @@
     mine = over_plane(copies(share, 16)).reshape(640, 128)
     other = lax.ppermute(mine, "gx", PAIR)
     core_block, block_peaks = core_of(core, mine, other, turned, start_plane)
-    return core_block.reshape(24, 16, 128), block_peaks
+    return core_block.reshape(24, 16, 128), block_peaks.T
 
 
 def solution(mesh):

time: 197 us -> 191 us (0.970)
  blocking collectives: 136 us -> 55.1 us
  waiting for transfers between devices: 10.5 us -> 78.9 us
  starting transfers between devices: 10.8 us -> 23.2 us
  local copies, waits for them, and re-layouts: 5.69 us -> 0.08 us
    all_to_all x1, blocking collectives: 91.1 us -> 10.3 us  [per_device(): grams = lax.all_to_all(copies(grams, 8), 'sp', 0, 0, tiled=True)]
    all_to_all x1, waiting for transfers between devices: 7.16 us -> 75.6 us  [per_device(): received = lax.all_to_all(sent, BOTH, 0, 0, tiled=True).reshape(8, 768, 128)]
    all_to_all x1, starting transfers between devices: 3.37 us -> 15.7 us  [per_device(): received = lax.all_to_all(sent, BOTH, 0, 0, tiled=True).reshape(8, 768, 128)]
    unnamed x14 -> x4, local copies, waits for them, and re-layouts: 4.97 us -> 0.01 us
where the time goes in v1:
time: 191 us
  waiting for transfers between devices  78.9 us (41%)
  blocking collectives  55.1 us (29%)
  Pallas kernels  32.6 us (17%)
  starting transfers between devices  23.2 us (12%)
    all_to_all x1, waiting for transfers between devices, per_device(): received = lax.all_to_all(sent, BOTH, 0, 0, tiled=True).reshape(8, 768, 128)  75.6 us
    all_to_all x3, blocking collectives, over_plane(): return lax.all_to_all(x, 'gx', 0, 0, tiled=True, axis_index_groups=PLANES)  34 us
    pallas_call x1, Pallas kernels, core_of(): pl.pallas_call(core_kernel, out_shape=(jax.ShapeDtypeStruct((384, 128), F...  16.4 us
    all_to_all x1, starting transfers between devices, per_device(): received = lax.all_to_all(sent, BOTH, 0, 0, tiled=True).reshape(8, 768, 128)  15.7 us
    all_to_all x1, blocking collectives, per_device(): lax.all_to_all(copies(share, 8), 'sp', 0, 0, tiled=True)  10.8 us
    all_to_all x1, blocking collectives, per_device(): grams = lax.all_to_all(copies(grams, 8), 'sp', 0, 0, tiled=True)  10.3 us
    pallas_call x1, Pallas kernels, plane_gram(): pl.pallas_call(plane_gram_kernel, out_shape=(jax.ShapeDtypeStruct((SPARE,...  8.75 us
    pallas_call x1, Pallas kernels, cells_first(): pl.pallas_call(cells_first_kernel, out_shape=jax.ShapeDtypeStruct((cells,...  3.9 us
  transfers between devices with their start and end apart: 4, of which 4 were waited for; matrix products, arithmetic and copies ran while one was open for 0% of the time, Pallas kernels for 0%

profile of v1, /device:TPU:1, one launch (start us, length us, event | category | flops | bytes accessed | tf_op | source)
XLA Modules:
  0.0 190.8 jit_solution(16920377585446745150)
XLA Ops:
  0.6 3.9 %shard_map.50 = f32[6144,128]{1,0:T(8,128)} custom-call(f32[128,6144]{1,0:T(8,128)} %bitcast.15), custom_call_target="tpu_custom_call" | custom-call | tf_op jit(solution)/shard_map/pallas_call | solution.py:194
  4.5 15.7 %all-to-all-start = ((f32[256,24,128]{2,1,0:T(8,128)}), f32[256,24,128]{2,1,0:T(8,128)S(1)}, u32[]{:S(2)}, u32[]{:S(2)}) async-start(f32[256,24,128]{2,1,0:T(8,128)} %bitcast.14), calls=%async_computation | async-start | bytes 6291456 | tf_op jit(solution)/shard_map/all_to_all | solution.py:395
  20.2 0.0 copy-start.1
  20.2 75.6 %all-to-all-done = f32[256,24,128]{2,1,0:T(8,128)S(1)} async-done(((f32[256,24,128]{2,1,0:T(8,128)}), f32[256,24,128]{2,1,0:T(8,128)S(1)}, u32[]{:S(2)}, u32[]{:S(2)}) %all-to-all-start) | async-done | bytes 3145760 | tf_op jit(solution)/shard_map/all_to_all | solution.py:395
  95.8 3.5 %shard_map.51 = f32[32,128]{1,0:T(8,128)S(1)} custom-call(f32[8,768,128]{2,1,0:T(8,128)S(1)} %bitcast.9), custom_call_target="tpu_custom_call" | custom-call | tf_op jit(solution)/shard_map/pallas_call | solution.py:247
  99.3 0.9 collective-permute-start
  100.2 0.8 collective-permute-done
  101.1 12.0 %all_to_all.30 = f32[16,32,128]{2,1,0:T(8,128)S(1)} all-to-all(f32[16,32,128]{2,1,0:T(8,128)S(1)} %broadcast_in_dim.8), channel_id=1, replica_groups={{0,2,4,6,8,10,12,14,16,18,20,22,24,26,28,30},{1,3,5,7,9,11,13,15,17,19,..., dimensions={0} | all-to-all | bytes 524288 | tf_op jit(solution)/shard_map/all_to_all | solution.py:385
  113.1 10.3 %all_to_all.31.g_ref = f32[8,32,128]{2,1,0:T(8,128)S(1)} all-to-all(f32[8,32,128]{2,1,0:T(8,128)S(1)} %broadcast_in_dim.9), channel_id=1, replica_groups=mesh['sp'=8,'gx'=32] {'sp'}, dimensions={0} | all-to-all | bytes 262144 | tf_op jit(solution)/shard_map/all_to_all | solution.py:399
  123.5 0.0 copy-done.1
  123.5 0.0 copy-start
  123.5 8.7 %shard_map.52 = (f32[32768,512]{1,0:T(8,128)}, f32[640,128]{1,0:T(8,128)S(1)}, f32[640,128]{1,0:T(8,128)S(1)}) custom-call(s32[1]{0:T(128)} %bitcast.3.core_ref, f32[8,768,128]{2,1,0:T(8,128)S(1)} %bitcast.10, f32[8,32,128]{2,1,0:T(8,128)S(1)} %all_to_all.31.g_ref, f32[16,64]{1,0:T(8,128)S(1)} %bitcast.13), custom_call_target="tpu_custom_call" | custom-call | tf_op jit(solution)/shard_map/pallas_call | solution.py:325
  132.2 2.7 %collective-permute-start.1 = (f32[640,128]{1,0:T(8,128)S(1)}, f32[640,128]{1,0:T(8,128)S(1)}, u32[]{:S(2)}, u32[]{:S(2)}) collective-permute-start(f32[640,128]{1,0:T(8,128)S(1)} %get-tuple-element.12), channel_id=1, source_target_pairs={{0,1},{1,0},{2,3},{3,2},{4,5},{5,4},{6,7},{7,6},{8,9},{9,8},{10,11... | collective-permute-start | bytes 983048 | tf_op jit(solution)/shard_map/ppermute | solution.py:401
  134.9 1.3 collective-permute-done.1
  136.2 11.4 %all_to_all.32 = f32[16,40,128]{2,1,0:T(8,128)S(1)} all-to-all(f32[16,40,128]{2,1,0:T(8,128)S(1)} %bitcast.16), channel_id=1, replica_groups={{0,2,4,6,8,10,12,14,16,18,20,22,24,26,28,30},{1,3,5,7,9,11,13,15,17,19,..., dimensions={0} | all-to-all | bytes 655360 | tf_op jit(solution)/shard_map/all_to_all | solution.py:385
  147.7 10.8 %all_to_all.33 = f32[8,40,128]{2,1,0:T(8,128)S(1)} all-to-all(f32[8,40,128]{2,1,0:T(8,128)S(1)} %broadcast_in_dim.10), channel_id=1, replica_groups=mesh['sp'=8,'gx'=32] {'sp'}, dimensions={0} | all-to-all | bytes 327680 | tf_op jit(solution)/shard_map/all_to_all | solution.py:403
  158.5 10.6 %all_to_all.34 = f32[16,40,128]{2,1,0:T(8,128)S(1)} all-to-all(f32[16,40,128]{2,1,0:T(8,128)S(1)} %broadcast_in_dim.11), channel_id=1, replica_groups={{0,2,4,6,8,10,12,14,16,18,20,22,24,26,28,30},{1,3,5,7,9,11,13,15,17,19,..., dimensions={0} | all-to-all | bytes 655360 | tf_op jit(solution)/shard_map/all_to_all | solution.py:385
  169.1 3.9 %collective-permute-start.2 = (f32[640,128]{1,0:T(8,128)S(1)}, f32[640,128]{1,0:T(8,128)S(1)}, u32[]{:S(2)}, u32[]{:S(2)}) collective-permute-start(f32[640,128]{1,0:T(8,128)S(1)} %bitcast.11), channel_id=1, source_target_pairs={{0,1},{1,0},{2,3},{3,2},{4,5},{5,4},{6,7},{7,6},{8,9},{9,8},{10,11... | collective-permute-start | bytes 983048 | tf_op jit(solution)/shard_map/ppermute | solution.py:405
  173.0 1.3 collective-permute-done.2.other_ref
  174.2 0.0 copy-done
  174.3 16.4 %shard_map.53 = (f32[384,128]{1,0:T(8,128)}, f32[16,24]{1,0:T(8,128)}) custom-call(s32[1]{0:T(128)} %bitcast.3.core_ref, f32[640,128]{1,0:T(8,128)S(1)} %bitcast.12, f32[640,128]{1,0:T(8,128)S(1)} %collective-permute-done.2.other_ref, f32[32768,512]{1,0:T(8,128)} %get-tuple-element.13.turned_hbm, f32[512,128]{1,0:T(8,128)S(1)} %copy-done), custom_call_target="tpu_custom_call" | custom-call | tf_op jit(solution)/shard_map/pallas_call | solution.py:375
  (9 shorter events, 0.2 us)
Async XLA Ops:
  4.5 91.3 %all-to-all-start = ((f32[256,24,128]{2,1,0:T(8,128)}), f32[256,24,128]{2,1,0:T(8,128)S(1)}, u32[]{:S(2)}, u32[]{:S(2)}) async-start(f32[256,24,128]{2,1,0:T(8,128)} %bitcast.14), calls=%async_computation | async-start | bytes 6291456 | tf_op jit(solution)/shard_map/all_to_all | solution.py:395
  20.2 103.3 %copy-start.1 = (f32[64,16]{0,1:T(8,128)S(1)}, f32[64,16]{0,1:T(8,128)}, u32[]{:S(2)}) copy-start(f32[64,16]{0,1:T(8,128)} %param.4) | copy-start | bytes 12292
  99.3 1.7 collective-permute-start
  123.5 50.8 %copy-start = (f32[512,128]{1,0:T(8,128)S(1)}, f32[512,128]{1,0:T(8,128)}, u32[]{:S(2)}) copy-start(f32[512,128]{1,0:T(8,128)} %start_ref.1) | copy-start | bytes 786436
  132.2 4.0 %collective-permute-start.1 = (f32[640,128]{1,0:T(8,128)S(1)}, f32[640,128]{1,0:T(8,128)S(1)}, u32[]{:S(2)}, u32[]{:S(2)}) collective-permute-start(f32[640,128]{1,0:T(8,128)S(1)} %get-tuple-element.12), channel_id=1, source_target_pairs={{0,1},{1,0},{2,3},{3,2},{4,5},{5,4},{6,7},{7,6},{8,9},{9,8},{10,11... | collective-permute-start | bytes 983048 | tf_op jit(solution)/shard_map/ppermute | solution.py:401
  169.1 5.2 %collective-permute-start.2 = (f32[640,128]{1,0:T(8,128)S(1)}, f32[640,128]{1,0:T(8,128)S(1)}, u32[]{:S(2)}, u32[]{:S(2)}) collective-permute-start(f32[640,128]{1,0:T(8,128)S(1)} %bitcast.11), channel_id=1, source_target_pairs={{0,1},{1,0},{2,3},{3,2},{4,5},{5,4},{6,7},{7,6},{8,9},{9,8},{10,11... | collective-permute-start | bytes 983048 | tf_op jit(solution)/shard_map/ppermute | solution.py:405

commit v2 on v1

--- a/solution.py
+++ b/solution.py
@@ -6,7 +6,6 @@
 from jax.sharding import PartitionSpec as P
 
 SWEEPS = 4
-HEIGHT = 2
 CHUNKS = 4
 SPARE = 32768
 F32 = jnp.float32
@@ -71,62 +70,83 @@
     return jnp.broadcast_to(x[i : i + 1, :], (8, 128))
 
 
-def inverse_factor(panels, height=1, between=None):
-    count = len(panels)
+def inverse_factor(tiles, between=None):
+    count = len(tiles)
     sub = lax.broadcasted_iota(jnp.int32, (8, 128), 0)
     lane = lax.broadcasted_iota(jnp.int32, (8, 128), 1)
-    state = list(panels)
+    state = list(tiles)
     result = []
-    for p in range(0, count, height):
-        width = 8 * height
-        own = (lane >= 8 * p) & (lane < 8 * p + width)
-        cols = [[across(state[p + t], 8 * p + j) for t in range(height)] for j in range(width)]
-        solved = [
-            jnp.where(own, jnp.where(lane == sub + 8 * (p + t), 1.0, 0.0), state[p + t]) for t in range(height)
-        ]
-        rows = [jnp.where(lane < 8 * p + width, x, 0.0) for x in solved]
-        root = [None] * height
-        diag = full_row(cols[0][0], 0)
-        for j in range(width):
-            tj, ij = divmod(j, 8)
+    for p in range(0, count, 2):
+        at = 8 * p
+        own_a, own_b = (lane >= at) & (lane < at + 8), (lane >= at + 8) & (lane < at + 16)
+        unit_a = jnp.where(lane == sub + at, 1.0, 0.0)
+        unit_b = jnp.where(lane == sub + at + 8, 1.0, 0.0)
+        cols = [across(state[p], at + j) for j in range(8)]
+        below = [across(state[p + 1], at + j) for j in range(8)]
+        right = [across(state[p + 1], at + 8 + j) for j in range(8)]
+        top = jnp.where(own_a, unit_a, state[p])
+        low = jnp.where(own_a, 0.0, state[p + 1])
+        diag = full_row(cols[0], 0)
+        for j in range(8):
             recip = 1.0 / diag
-            pivots = [full_row(cols[k][tj], ij) for k in range(j + 1, width)]
-            if j + 1 < width:
-                tn, i_n = divmod(j + 1, 8)
-                diag = full_row(cols[j + 1][tn], i_n) - (full_row(cols[j][tn], i_n) * pivots[0]) * recip
-            root[tj] = recip if ij == 0 else jnp.where(sub == ij, recip, root[tj])
-            mult = []
-            for t in range(height):
-                m = cols[j][t] * recip
-                mult.append(jnp.where(sub == ij, 0.0, m) if t == tj else m)
-            for k in range(j + 1, width):
-                cols[k] = [cols[k][t] - mult[t] * pivots[k - j - 1] for t in range(height)]
-            pivot = full_row(solved[tj], ij)
-            solved = [solved[t] - mult[t] * pivot for t in range(height)]
-            pivot = full_row(rows[tj], ij)
-            for t in range(tj, height):
-                m = jnp.where(sub > ij, mult[t], 0.0) if t == tj else mult[t]
-                rows[t] = rows[t] - m * pivot
-        for t in range(height):
-            result.append(rows[t] * jnp.sqrt(root[t]))
-            solved[t] = solved[t] * root[t]
-        near = min(p + 2 * height, count)
-        for k in range(p + height, near):
-            fresh = jnp.where(own, 0.0, state[k])
-            for j in range(width):
-                tj, ij = divmod(j, 8)
-                fresh = fresh - across(state[k], 8 * p + j) * full_row(solved[tj], ij)
-            state[k] = fresh
+            pivots = [full_row(cols[k], j) for k in range(j + 1, 8)]
+            crossing = [full_row(below[j], k) for k in range(8)]
+            if j < 7:
+                diag = full_row(cols[j + 1], j + 1) - (full_row(cols[j], j + 1) * pivots[0]) * recip
+            else:
+                diag = full_row(right[0], 0) - (crossing[0] * crossing[0]) * recip
+            root_a = recip if j == 0 else jnp.where(sub == j, recip, root_a)
+            up = jnp.where(sub == j, 0.0, cols[j] * recip)
+            down = below[j] * recip
+            for k in range(j + 1, 8):
+                cols[k] = cols[k] - up * pivots[k - j - 1]
+                below[k] = below[k] - down * pivots[k - j - 1]
+            for k in range(8):
+                right[k] = right[k] - down * crossing[k]
+            forward_a = top if j == 0 else jnp.where(sub == j, top, forward_a)
+            pivot = full_row(top, j)
+            top, low = top - up * pivot, low - down * pivot
+        top = top * root_a
+        mixed = [across(top, at + 8 + k) for k in range(8)]
+        top = jnp.where(own_b, 0.0, top)
+        low = jnp.where(own_b, unit_b, low)
+        for j in range(8):
+            recip = 1.0 / diag
+            pivots = [full_row(right[k], j) for k in range(j + 1, 8)]
+            if j < 7:
+                diag = full_row(right[j + 1], j + 1) - (full_row(right[j], j + 1) * pivots[0]) * recip
+            root_b = recip if j == 0 else jnp.where(sub == j, recip, root_b)
+            up = jnp.where(sub == j, 0.0, right[j] * recip)
+            for k in range(j + 1, 8):
+                right[k] = right[k] - up * pivots[k - j - 1]
+            forward_b = low if j == 0 else jnp.where(sub == j, low, forward_b)
+            low = low - up * full_row(low, j)
+        low = low * root_b
+        result.append(jnp.where(lane < at + 8, forward_a * jnp.sqrt(root_a), 0.0))
+        result.append(jnp.where(lane < at + 16, forward_b * jnp.sqrt(root_b), 0.0))
+        low_rows = [full_row(low, k) for k in range(8)]
+        for k in range(8):
+            top = top - mixed[k] * low_rows[k]
+        own = own_a | own_b
+        near = min(p + 4, count)
+        for k in range(p + 2, near):
+            one = jnp.where(own, 0.0, state[k])
+            for j in range(8):
+                one = one - across(state[k], at + 8 + j) * low_rows[j]
+            two = across(state[k], at) * full_row(top, 0)
+            for j in range(1, 8):
+                two = two + across(state[k], at + j) * full_row(top, j)
+            state[k] = one - two
         if near < count:
             far = jnp.concatenate(state[near:], axis=0)
-            ends = [jnp.zeros((8 * n, 128), F32) for n in (p, 16 - p - height)]
-            weights = jnp.concatenate(([ends[0]] if p else []) + solved + [ends[1]], axis=0)
+            ends = [jnp.zeros((8 * n, 128), F32) for n in (p, 14 - p)]
+            weights = jnp.concatenate(([ends[0]] if p else []) + [top, low, ends[1]], axis=0)
             change = six(split3(far), split3(weights))
             for k in range(near, count):
-                at = 8 * (k - near)
-                state[k] = jnp.where(own, 0.0, state[k]) - change[at : at + 8]
+                rows = slice(8 * (k - near), 8 * (k - near) + 8)
+                state[k] = jnp.where(own, 0.0, state[k]) - change[rows]
         if between is not None:
-            between(p // height)
+            between(p // 2)
     return result
 
 
@@ -145,7 +165,7 @@
                 image_ref[rows, :] = six(tuple(g[rows] for g in split_gram), pieces)
 
         tiles = [inner[8 * p : 8 * p + 8] for p in range(16)]
-        factor = split3(jnp.concatenate(inverse_factor(tiles, HEIGHT, ahead), axis=0))
+        factor = split3(jnp.concatenate(inverse_factor(tiles, ahead), axis=0))
         image_block = six(pieces if last else split3(image_ref[...]), factor, NT)
     return image_block
 
@@ -159,7 +179,7 @@
         inner = six_gram(pieces)
         ahead = pieces if sweep + 1 == SWEEPS else split3(six(split_gram, pieces))
         between(sweep)
-        factor = inverse_factor([inner[0:8], inner[8:16]], 2)
+        factor = inverse_factor([inner[0:8], inner[8:16]])
         image_block = six(ahead, split3(jnp.concatenate(factor + [blank], axis=0)), NT)
     return image_block
 
@@ -167,14 +187,9 @@
 STEPS = 8
 
 
-def cells_first_kernel(x_ref, o_ref, tile_ref, turned_ref, in_sems, out_sems):
+def cells_first_kernel(x_ref, o_ref, tile_ref, sems):
     step = o_ref.shape[0] // STEPS
-    loads = [
-        pltpu.make_async_copy(x_ref.at[:, pl.ds(step * k, step)], tile_ref.at[k], in_sems.at[k]) for k in range(STEPS)
-    ]
-    stores = [
-        pltpu.make_async_copy(turned_ref.at[k], o_ref.at[pl.ds(step * k, step)], out_sems.at[k]) for k in range(STEPS)
-    ]
+    loads = [pltpu.make_async_copy(x_ref.at[:, pl.ds(step * k, step)], tile_ref.at[k], sems.at[k]) for k in range(STEPS)]
     for load in loads:
         load.start()
     for k in range(STEPS):
@@ -182,10 +197,8 @@
         for n in range(step // 128):
             tile = tile_ref[k, :, 128 * n : 128 * (n + 1)].reshape(8, 16, 128)
             rows = jnp.concatenate([tile[:, x, :] for x in range(16)], axis=0)
-            turned_ref[k, 128 * n : 128 * (n + 1), :] = rows.T
-        stores[k].start()
-    for store in stores:
-        store.wait()
+            at = step * k + 128 * n
+            o_ref[at : at + 128, :] = rows.T
 
 
 def cells_first(block):
@@ -195,21 +208,16 @@
         cells_first_kernel,
         out_shape=jax.ShapeDtypeStruct((cells, 128), F32),
         in_specs=[pl.BlockSpec(memory_space=pltpu.HBM)],
-        out_specs=pl.BlockSpec(memory_space=pltpu.HBM),
-        scratch_shapes=[
-            pltpu.VMEM((STEPS, 128, step), F32),
-            pltpu.VMEM((STEPS, step, 128), F32),
-            pltpu.SemaphoreType.DMA((STEPS,)),
-            pltpu.SemaphoreType.DMA((STEPS,)),
-        ],
-        compiler_params=grant(56),
+        out_specs=pl.BlockSpec(memory_space=pltpu.VMEM),
+        scratch_shapes=[pltpu.VMEM((STEPS, 128, step), F32), pltpu.SemaphoreType.DMA((STEPS,))],
+        compiler_params=grant(50),
     )(block.reshape(128, cells))
 
 
 def species_gram_kernel(r_ref, o_ref, ht_ref, h_ref, l_ref):
     for s in range(8):
         high, low = split2(r_ref[s])
-        ht_ref[128 * s : 128 * (s + 1), :] = r_ref[s].T.astype(BF16)
+        ht_ref[128 * s : 128 * (s + 1), :] = high.T
         h_ref[:, 128 * s : 128 * (s + 1)] = high
         l_ref[:, 128 * s : 128 * (s + 1)] = low
     lane = lax.broadcasted_iota(jnp.int32, (8, 256), 1) % 128
@@ -257,7 +265,7 @@
 
 
 def plane_gram_kernel(
-    core_ref, r_ref, g_ref, start_ref, out_ref, mine_ref, other_ref, wh_ref, wl_ref, h_ref, l_ref, red_ref, turned_ref, sem
+    r_ref, g_ref, start_ref, out_ref, mine_ref, other_ref, wh_ref, wl_ref, h_ref, l_ref, red_ref, turned_ref, sem
 ):
     def between(sweep):
         for s in (2 * sweep, 2 * sweep + 1):
@@ -268,8 +276,9 @@
     gram = jnp.concatenate([folded[:, 0:64], folded[:, 64:128]], axis=0)
     start = jnp.concatenate([start_ref[...], jnp.zeros((112, 64), F32)], axis=0).T
     basis = subspace_narrow(gram, start, between)[:, 0:16]
+    column = lax.broadcasted_iota(jnp.int32, (16, 256), 1)
     widen = jnp.where(
-        lax.broadcasted_iota(jnp.int32, (16, 256), 1) // 16 == lax.broadcasted_iota(jnp.int32, (16, 256), 0), 1.0, 0.0
+        column // 16 % 4 * 4 + column // 64 == lax.broadcasted_iota(jnp.int32, (16, 256), 0), 1.0, 0.0
     ).astype(BF16)
     high, mid, low = split3(basis)
     wide = bf16_dot(jnp.concatenate([high, mid, low], axis=1), jnp.concatenate([widen] * 3, axis=0))
@@ -284,34 +293,39 @@
     wh = wh_ref[...]
     total = bf16_dot(h_ref[...], wh) + (bf16_dot(h_ref[...], wl_ref[...]) + bf16_dot(l_ref[...], wh))
     red_ref[...] = total
-    lane = lax.broadcasted_iota(jnp.int32, (16, 128), 1)
-    blank = jnp.zeros((8, 256), F32)
-    for a in range(8):
+    lane = lax.broadcasted_iota(jnp.int32, (24, 128), 1)
+    blank = jnp.zeros((8, 128), F32)
+    for pair in range(16):
         rows = []
-        for b in range(4):
-            g = 4 * a + b
-            rows += [red_ref[24 * g : 24 * g + 24, :], blank]
+        for k in range(4):
+            lanes = slice(128 * (k // 2), 128 * (k // 2 + 1))
+            at = 48 * pair
+            first, second = red_ref[at : at + 24, lanes], red_ref[at + 24 : at + 48, lanes]
+            if k % 2:
+                first = pltpu.roll(first, 64, 1)
+            else:
+                second = pltpu.roll(second, 64, 1)
+            rows += [jnp.where(lane < 64, first, second), blank]
         turned = jnp.concatenate(rows, axis=0).T
-        shifted = [turned] + [pltpu.roll(turned, 32 * k, 1) for k in range(1, 4)]
-        for b in range(4):
-            g = 4 * a + b
-            for quad in range(4):
-                block = None
-                for k in range(4):
-                    r = 4 * quad + k
-                    piece = shifted[(k - b) % 4][16 * r : 16 * r + 16, :]
-                    block = piece if k == 0 else jnp.where(lane // 32 == k, piece, block)
-                turned_ref[16 * g : 16 * g + 16, 128 * quad : 128 * (quad + 1)] = block
+        for g in range(2):
+            for q in range(4):
+                at, to = 64 * g + 16 * q, 32 * pair + 16 * g
+                turned_ref[to : to + 16, 128 * q : 128 * (q + 1)] = turned[at : at + 16]
     copy = pltpu.make_async_copy(turned_ref, out_ref.at[pl.ds(0, 512)], sem)
     copy.start()
     high, low = split2(turned_ref[...])
     left = jnp.concatenate([high, high, low], axis=1)
     right = jnp.concatenate([high, low, high], axis=1)
+    quarter = [slice(0, 256), slice(256, 512)]
+    whole = {
+        (i, j): bf16_dot(left[quarter[i]], right[quarter[j]], NT) for i, j in ((0, 0), (0, 1), (1, 1))
+    }
     blocks = []
     for i in range(4):
         for j in range(i, 4):
-            blocks.append(bf16_dot(left[128 * i : 128 * (i + 1)], right[128 * j : 128 * (j + 1)], NT))
-    first = core_ref[0] == 0
+            rows, lanes = slice(128 * (i % 2), 128 * (i % 2 + 1)), slice(128 * (j % 2), 128 * (j % 2 + 1))
+            blocks.append(whole[i // 2, j // 2][rows, lanes])
+    first = lax.axis_index("gx") % 2 == 0
     for n in range(5):
         rows = slice(128 * n, 128 * (n + 1))
         mine_ref[rows, :] = jnp.where(first, blocks[n], blocks[n + 5])
@@ -319,13 +333,13 @@
     copy.wait()
 
 
-def plane_gram(core, received, grams, start_species):
+def plane_gram(received, grams, start_species):
     half = jax.ShapeDtypeStruct((640, 128), F32)
     whole = pl.BlockSpec(memory_space=pltpu.VMEM)
     return pl.pallas_call(
         plane_gram_kernel,
         out_shape=(jax.ShapeDtypeStruct((SPARE, 512), F32), half, half),
-        in_specs=[pl.BlockSpec(memory_space=pltpu.SMEM), whole, whole, whole],
+        in_specs=[whole, whole, whole],
         out_specs=(pl.BlockSpec(memory_space=pltpu.HBM), whole, whole),
         scratch_shapes=[
             pltpu.VMEM((1024, 256), BF16),
@@ -337,15 +351,15 @@
             pltpu.SemaphoreType.DMA,
         ],
         compiler_params=grant(20),
-    )(core, received, grams, start_species.T)
+    )(received, grams, start_species.T)
 
 
 def core_kernel(
-    core_ref, mine_ref, other_ref, turned_hbm, start_ref, out_ref, peaks_ref, image_ref, turned_ref, sem
+    mine_ref, other_ref, turned_hbm, start_ref, out_ref, peaks_ref, image_ref, turned_ref, sem
 ):
     copy = pltpu.make_async_copy(turned_hbm.at[pl.ds(0, 512)], turned_ref, sem)
     copy.start()
-    first = core_ref[0] == 0
+    first = lax.axis_index("gx") % 2 == 0
     blocks = {}
     n = 0
     for i in range(4):
@@ -370,15 +384,15 @@
     peaks_ref[...] = peaks[:, 0:24]
 
 
-def core_of(core, mine, other, turned, start_plane):
+def core_of(mine, other, turned, start_plane):
     whole = pl.BlockSpec(memory_space=pltpu.VMEM)
     return pl.pallas_call(
         core_kernel,
         out_shape=(jax.ShapeDtypeStruct((384, 128), F32), jax.ShapeDtypeStruct((16, 24), F32)),
-        in_specs=[pl.BlockSpec(memory_space=pltpu.SMEM), whole, whole, pl.BlockSpec(memory_space=pltpu.HBM), whole],
+        in_specs=[whole, whole, pl.BlockSpec(memory_space=pltpu.HBM), whole],
         scratch_shapes=[pltpu.VMEM((512, 128), F32), pltpu.VMEM((512, 512), F32), pltpu.SemaphoreType.DMA],
         compiler_params=grant(20),
-    )(core, mine, other, turned, start_plane)
+    )(mine, other, turned, start_plane)
 
 
 def over_plane(x):
@@ -390,20 +404,19 @@
 
 
 def per_device(tensor, start_species, start_plane):
-    core = (lax.axis_index("gx") % 2).astype(jnp.int32).reshape(1)
     sent = cells_first(tensor).reshape(256, 24, 128)
     received = lax.all_to_all(sent, BOTH, 0, 0, tiled=True).reshape(8, 768, 128)
-    grams, core = lax.optimization_barrier((species_gram(received), core))
+    grams = species_gram(received)
     grams = grams + lax.ppermute(grams, "gx", PAIR)
     grams = jnp.sum(over_plane(copies(grams, 16)), axis=0)
     grams = lax.all_to_all(copies(grams, 8), "sp", 0, 0, tiled=True)
-    turned, mine, other = plane_gram(core, received, grams, start_species)
+    turned, mine, other = plane_gram(received, grams, start_species)
     mine = mine + lax.ppermute(other, "gx", PAIR)
     share = jnp.sum(over_plane(mine.reshape(16, 40, 128)), axis=0)
     share = jnp.sum(lax.all_to_all(copies(share, 8), "sp", 0, 0, tiled=True), axis=0)
     mine = over_plane(copies(share, 16)).reshape(640, 128)
     other = lax.ppermute(mine, "gx", PAIR)
-    core_block, block_peaks = core_of(core, mine, other, turned, start_plane)
+    core_block, block_peaks = core_of(mine, other, turned, start_plane)
     return core_block.reshape(24, 16, 128), block_peaks.T
 
 

time: 191 us -> 189 us (0.990)
  blocking collectives: 55.1 us -> 147 us
  waiting for transfers between devices: 78.9 us -> 3.35 us
  starting transfers between devices: 23.2 us -> 7.56 us
  Pallas kernels: 32.6 us -> 29.1 us
    all_to_all x0 -> x1, blocking collectives: none -> 91.1 us  [per_device(): received = lax.all_to_all(sent, BOTH, 0, 0, tiled=True).reshape(8, 768, 128)]
    all_to_all x1 -> x0, waiting for transfers between devices: 75.6 us -> none  [per_device(): received = lax.all_to_all(sent, BOTH, 0, 0, tiled=True).reshape(8, 768, 128)]
    all_to_all x1 -> x0, starting transfers between devices: 15.7 us -> none  [per_device(): received = lax.all_to_all(sent, BOTH, 0, 0, tiled=True).reshape(8, 768, 128)]
  transfers between devices with their start and end apart: 4 -> 3, of which waited for: 4 -> 3; matrix products, arithmetic and copies ran while one was open for 0% -> 0% of each run, Pallas kernels for 0% -> 0%
where the time goes in v2:
time: 189 us
  blocking collectives  147 us (78%)
  Pallas kernels  29.1 us (15%)
  starting transfers between devices  7.56 us (4%)
  waiting for transfers between devices  3.35 us (2%)
    all_to_all x1, blocking collectives, per_device(): received = lax.all_to_all(sent, BOTH, 0, 0, tiled=True).reshape(8, 768, 128)  91.1 us
    all_to_all x3, blocking collectives, over_plane(): return lax.all_to_all(x, 'gx', 0, 0, tiled=True, axis_index_groups=PLANES)  34.1 us
    pallas_call x1, Pallas kernels, core_of(): pl.pallas_call(core_kernel, out_shape=(jax.ShapeDtypeStruct((384, 128), F...  15.4 us
    all_to_all x1, blocking collectives, per_device(): grams = lax.all_to_all(copies(grams, 8), 'sp', 0, 0, tiled=True)  10.9 us
    all_to_all x1, blocking collectives, per_device(): lax.all_to_all(copies(share, 8), 'sp', 0, 0, tiled=True)  10.8 us
    pallas_call x1, Pallas kernels, plane_gram(): pl.pallas_call(plane_gram_kernel, out_shape=(jax.ShapeDtypeStruct((SPARE,...  7.2 us
    ppermute x1, starting transfers between devices, per_device(): other = lax.ppermute(mine, 'gx', PAIR)  3.9 us
  transfers between devices with their start and end apart: 3, of which 3 were waited for; matrix products, arithmetic and copies ran while one was open for 0% of the time, Pallas kernels for 0%

profile of v2, /device:TPU:1, one launch (start us, length us, event | category | flops | bytes accessed | tf_op | source)
XLA Modules:
  0.0 188.8 jit_solution(184540987481383578)
XLA Ops:
  0.6 3.1 %shard_map.50 = f32[6144,128]{1,0:T(8,128)S(1)} custom-call(f32[128,6144]{1,0:T(8,128)} %bitcast.14), custom_call_target="tpu_custom_call" | custom-call | tf_op jit(solution)/shard_map/pallas_call | solution.py:207
  3.7 91.1 %all_to_all.30 = f32[256,24,128]{2,1,0:T(8,128)S(1)} all-to-all(f32[256,24,128]{2,1,0:T(8,128)S(1)} %bitcast.10), channel_id=1, replica_groups=mesh['sp'=8,'gx'=32] {'sp','gx'}, dimensions={0} | all-to-all | bytes 6291456 | tf_op jit(solution)/shard_map/all_to_all | solution.py:408
  94.8 0.0 copy-start.1
  94.8 3.4 %shard_map.51 = f32[32,128]{1,0:T(8,128)S(1)} custom-call(f32[8,768,128]{2,1,0:T(8,128)S(1)} %bitcast.8), custom_call_target="tpu_custom_call" | custom-call | tf_op jit(solution)/shard_map/pallas_call | solution.py:255
  98.2 0.9 collective-permute-start
  99.1 0.8 collective-permute-done
  100.0 12.1 %all_to_all.31 = f32[16,32,128]{2,1,0:T(8,128)} all-to-all(f32[16,32,128]{2,1,0:T(8,128)S(1)} %broadcast_in_dim.8), channel_id=1, replica_groups={{0,2,4,6,8,10,12,14,16,18,20,22,24,26,28,30},{1,3,5,7,9,11,13,15,17,19,..., dimensions={0} | all-to-all | bytes 524288 | tf_op jit(solution)/shard_map/all_to_all | solution.py:399
  112.0 1.0 reduce_sum.27
  113.0 10.9 %all_to_all.32.g_ref = f32[8,32,128]{2,1,0:T(8,128)S(1)} all-to-all(f32[8,32,128]{2,1,0:T(8,128)S(1)} %broadcast_in_dim.9), channel_id=1, replica_groups=mesh['sp'=8,'gx'=32] {'sp'}, dimensions={0} | all-to-all | bytes 262144 | tf_op jit(solution)/shard_map/all_to_all | solution.py:412
  123.9 0.0 copy-done.1
  123.9 0.0 copy-start
  123.9 7.2 %shard_map.52 = (f32[32768,512]{1,0:T(8,128)}, f32[640,128]{1,0:T(8,128)S(1)}, f32[640,128]{1,0:T(8,128)S(1)}) custom-call(f32[8,768,128]{2,1,0:T(8,128)S(1)} %bitcast.9, f32[8,32,128]{2,1,0:T(8,128)S(1)} %all_to_all.32.g_ref, f32[16,64]{1,0:T(8,128)S(1)} %bitcast.13), custom_call_target="tpu_custom_call" | custom-call | tf_op jit(solution)/shard_map/pallas_call | solution.py:339
  131.1 2.8 %collective-permute-start.1 = (f32[640,128]{1,0:T(8,128)S(1)}, f32[640,128]{1,0:T(8,128)S(1)}, u32[]{:S(2)}, u32[]{:S(2)}) collective-permute-start(f32[640,128]{1,0:T(8,128)S(1)} %get-tuple-element.8), channel_id=1, source_target_pairs={{0,1},{1,0},{2,3},{3,2},{4,5},{5,4},{6,7},{7,6},{8,9},{9,8},{10,11... | collective-permute-start | bytes 983048 | tf_op jit(solution)/shard_map/ppermute | solution.py:414
  133.9 1.3 collective-permute-done.1
  135.2 11.4 %all_to_all.33 = f32[16,40,128]{2,1,0:T(8,128)S(1)} all-to-all(f32[16,40,128]{2,1,0:T(8,128)S(1)} %bitcast.15), channel_id=1, replica_groups={{0,2,4,6,8,10,12,14,16,18,20,22,24,26,28,30},{1,3,5,7,9,11,13,15,17,19,..., dimensions={0} | all-to-all | bytes 655360 | tf_op jit(solution)/shard_map/all_to_all | solution.py:399
  146.7 10.8 %all_to_all.34 = f32[8,40,128]{2,1,0:T(8,128)S(1)} all-to-all(f32[8,40,128]{2,1,0:T(8,128)S(1)} %broadcast_in_dim.10), channel_id=1, replica_groups=mesh['sp'=8,'gx'=32] {'sp'}, dimensions={0} | all-to-all | bytes 327680 | tf_op jit(solution)/shard_map/all_to_all | solution.py:416
  157.5 10.6 %all_to_all.35 = f32[16,40,128]{2,1,0:T(8,128)S(1)} all-to-all(f32[16,40,128]{2,1,0:T(8,128)S(1)} %broadcast_in_dim.11), channel_id=1, replica_groups={{0,2,4,6,8,10,12,14,16,18,20,22,24,26,28,30},{1,3,5,7,9,11,13,15,17,19,..., dimensions={0} | all-to-all | bytes 655360 | tf_op jit(solution)/shard_map/all_to_all | solution.py:399
  168.1 3.9 %collective-permute-start.2 = (f32[640,128]{1,0:T(8,128)S(1)}, f32[640,128]{1,0:T(8,128)S(1)}, u32[]{:S(2)}, u32[]{:S(2)}) collective-permute-start(f32[640,128]{1,0:T(8,128)S(1)} %bitcast.11), channel_id=1, source_target_pairs={{0,1},{1,0},{2,3},{3,2},{4,5},{5,4},{6,7},{7,6},{8,9},{9,8},{10,11... | collective-permute-start | bytes 983048 | tf_op jit(solution)/shard_map/ppermute | solution.py:418
  172.0 1.3 collective-permute-done.2.other_ref
  173.2 0.0 copy-done
  173.2 15.4 %shard_map.53 = (f32[384,128]{1,0:T(8,128)}, f32[16,24]{1,0:T(8,128)}) custom-call(f32[640,128]{1,0:T(8,128)S(1)} %bitcast.12, f32[640,128]{1,0:T(8,128)S(1)} %collective-permute-done.2.other_ref, f32[32768,512]{1,0:T(8,128)} %get-tuple-element.9.turned_hbm, f32[512,128]{1,0:T(8,128)S(1)} %copy-done), custom_call_target="tpu_custom_call" | custom-call | tf_op jit(solution)/shard_map/pallas_call | solution.py:389
  (8 shorter events, 0.2 us)
Async XLA Ops:
  94.8 29.2 %copy-start.1 = (f32[64,16]{0,1:T(8,128)S(1)}, f32[64,16]{0,1:T(8,128)}, u32[]{:S(2)}) copy-start(f32[64,16]{0,1:T(8,128)} %param.4) | copy-start | bytes 12292
  98.2 1.7 collective-permute-start
  123.9 49.3 %copy-start = (f32[512,128]{1,0:T(8,128)S(1)}, f32[512,128]{1,0:T(8,128)}, u32[]{:S(2)}) copy-start(f32[512,128]{1,0:T(8,128)} %start_ref.1) | copy-start | bytes 786436
  131.1 4.0 %collective-permute-start.1 = (f32[640,128]{1,0:T(8,128)S(1)}, f32[640,128]{1,0:T(8,128)S(1)}, u32[]{:S(2)}, u32[]{:S(2)}) collective-permute-start(f32[640,128]{1,0:T(8,128)S(1)} %get-tuple-element.8), channel_id=1, source_target_pairs={{0,1},{1,0},{2,3},{3,2},{4,5},{5,4},{6,7},{7,6},{8,9},{9,8},{10,11... | collective-permute-start | bytes 983048 | tf_op jit(solution)/shard_map/ppermute | solution.py:414
  168.1 5.2 %collective-permute-start.2 = (f32[640,128]{1,0:T(8,128)S(1)}, f32[640,128]{1,0:T(8,128)S(1)}, u32[]{:S(2)}, u32[]{:S(2)}) collective-permute-start(f32[640,128]{1,0:T(8,128)S(1)} %bitcast.11), channel_id=1, source_target_pairs={{0,1},{1,0},{2,3},{3,2},{4,5},{5,4},{6,7},{7,6},{8,9},{9,8},{10,11... | collective-permute-start | bytes 983048 | tf_op jit(solution)/shard_map/ppermute | solution.py:418

commit v3 on v2

--- a/solution.py
+++ b/solution.py
@@ -248,13 +248,15 @@
     ).astype(F32)
     half = exact_dot(wide, fold)
     gram = half + half.T
-    o_ref[...] = jnp.concatenate([gram[0:32], gram[32:64]], axis=1)
+    second = jnp.concatenate([gram[48:64, 48:64], gram[16:32, 16:64]], axis=1)
+    rows = jnp.concatenate([gram[0:16], second, gram[32:48]], axis=0)
+    o_ref[...] = jnp.concatenate([rows[0:24], rows[24:48]], axis=1)
 
 
 def species_gram(received):
     return pl.pallas_call(
         species_gram_kernel,
-        out_shape=jax.ShapeDtypeStruct((32, 128), F32),
+        out_shape=jax.ShapeDtypeStruct((24, 128), F32),
         scratch_shapes=[
             pltpu.VMEM((1024, 768), BF16),
             pltpu.VMEM((768, 1024), BF16),
@@ -273,7 +275,13 @@
             h_ref[:, lanes], l_ref[:, lanes] = split2(r_ref[s])
 
     folded = jnp.sum(g_ref[...], axis=0)
-    gram = jnp.concatenate([folded[:, 0:64], folded[:, 64:128]], axis=0)
+    rows = jnp.concatenate([folded[:, 0:64], folded[:, 64:128]], axis=0)
+    across_rows = jnp.concatenate(
+        [jnp.concatenate([rows, jnp.zeros((80, 64), F32)], axis=0), jnp.zeros((128, 64), F32)], axis=1
+    ).T
+    second = jnp.concatenate([across_rows[16:32, 0:16], rows[16:32, 16:64]], axis=1)
+    last = jnp.concatenate([across_rows[48:64, 0:48], rows[16:32, 0:16]], axis=1)
+    gram = jnp.concatenate([rows[0:16], second, rows[32:48], last], axis=0)
     start = jnp.concatenate([start_ref[...], jnp.zeros((112, 64), F32)], axis=0).T
     basis = subspace_narrow(gram, start, between)[:, 0:16]
     column = lax.broadcasted_iota(jnp.int32, (16, 256), 1)
@@ -408,8 +416,8 @@
     received = lax.all_to_all(sent, BOTH, 0, 0, tiled=True).reshape(8, 768, 128)
     grams = species_gram(received)
     grams = grams + lax.ppermute(grams, "gx", PAIR)
-    grams = jnp.sum(over_plane(copies(grams, 16)), axis=0)
-    grams = lax.all_to_all(copies(grams, 8), "sp", 0, 0, tiled=True)
+    grams = jnp.sum(lax.all_to_all(copies(grams, 8), "sp", 0, 0, tiled=True), axis=0)
+    grams = over_plane(copies(grams, 16))
     turned, mine, other = plane_gram(received, grams, start_species)
     mine = mine + lax.ppermute(other, "gx", PAIR)
     share = jnp.sum(over_plane(mine.reshape(16, 40, 128)), axis=0)

time: 189 us -> 187 us (0.989)
  blocking collectives: 147 us -> 145 us
where the time goes in v3:
time: 187 us
  blocking collectives  145 us (78%)
  Pallas kernels  29.2 us (16%)
  starting transfers between devices  8.11 us (4%)
  waiting for transfers between devices  3.35 us (2%)
    all_to_all x1, blocking collectives, per_device(): received = lax.all_to_all(sent, BOTH, 0, 0, tiled=True).reshape(8, 768, 128)  91.1 us
    all_to_all x3, blocking collectives, over_plane(): return lax.all_to_all(x, 'gx', 0, 0, tiled=True, axis_index_groups=PLANES)  32.5 us
    pallas_call x1, Pallas kernels, core_of(): pl.pallas_call(core_kernel, out_shape=(jax.ShapeDtypeStruct((384, 128), F...  15.4 us
    all_to_all x1, blocking collectives, per_device(): lax.all_to_all(copies(share, 8), 'sp', 0, 0, tiled=True)  10.8 us
    all_to_all x1, blocking collectives, per_device(): lax.all_to_all(copies(grams, 8), 'sp', 0, 0, tiled=True)  10.7 us
    pallas_call x1, Pallas kernels, plane_gram(): pl.pallas_call(plane_gram_kernel, out_shape=(jax.ShapeDtypeStruct((SPARE,...  7.27 us
    ppermute x1, starting transfers between devices, per_device(): other = lax.ppermute(mine, 'gx', PAIR)  3.9 us
  transfers between devices with their start and end apart: 3, of which 3 were waited for; matrix products, arithmetic and copies ran while one was open for 0% of the time, Pallas kernels for 0%

profile of v3, /device:TPU:1, one launch (start us, length us, event | category | flops | bytes accessed | tf_op | source)
XLA Modules:
  0.0 186.7 jit_solution(13299106383106356247)
XLA Ops:
  0.6 3.1 %shard_map.50 = f32[6144,128]{1,0:T(8,128)S(1)} custom-call(f32[128,6144]{1,0:T(8,128)} %bitcast.14), custom_call_target="tpu_custom_call" | custom-call | tf_op jit(solution)/shard_map/pallas_call | solution.py:207
  3.7 91.1 %all_to_all.30 = f32[256,24,128]{2,1,0:T(8,128)S(1)} all-to-all(f32[256,24,128]{2,1,0:T(8,128)S(1)} %bitcast.10), channel_id=1, replica_groups=mesh['sp'=8,'gx'=32] {'sp','gx'}, dimensions={0} | all-to-all | bytes 6291456 | tf_op jit(solution)/shard_map/all_to_all | solution.py:416
  94.8 0.0 copy-start.1
  94.8 3.5 %shard_map.51 = f32[24,128]{1,0:T(8,128)S(1)} custom-call(f32[8,768,128]{2,1,0:T(8,128)S(1)} %bitcast.8), custom_call_target="tpu_custom_call" | custom-call | tf_op jit(solution)/shard_map/pallas_call | solution.py:257
  98.3 0.9 collective-permute-start
  99.1 0.8 collective-permute-done
  100.0 10.7 %all_to_all.31 = f32[8,24,128]{2,1,0:T(8,128)S(1)} all-to-all(f32[8,24,128]{2,1,0:T(8,128)S(1)} %broadcast_in_dim.8), channel_id=1, replica_groups=mesh['sp'=8,'gx'=32] {'sp'}, dimensions={0} | all-to-all | bytes 196608 | tf_op jit(solution)/shard_map/all_to_all | solution.py:419
  110.7 10.4 %all_to_all.32.g_ref = f32[16,24,128]{2,1,0:T(8,128)S(1)} all-to-all(f32[16,24,128]{2,1,0:T(8,128)S(1)} %broadcast_in_dim.9), channel_id=1, replica_groups={{0,2,4,6,8,10,12,14,16,18,20,22,24,26,28,30},{1,3,5,7,9,11,13,15,17,19,..., dimensions={0} | all-to-all | bytes 393216 | tf_op jit(solution)/shard_map/all_to_all | solution.py:407
  121.1 0.0 copy-done.1
  121.1 0.0 copy-start
  121.1 7.3 %shard_map.52 = (f32[32768,512]{1,0:T(8,128)}, f32[640,128]{1,0:T(8,128)S(1)}, f32[640,128]{1,0:T(8,128)S(1)}) custom-call(f32[8,768,128]{2,1,0:T(8,128)S(1)} %bitcast.9, f32[16,24,128]{2,1,0:T(8,128)S(1)} %all_to_all.32.g_ref, f32[16,64]{1,0:T(8,128)S(1)} %bitcast.13), custom_call_target="tpu_custom_call" | custom-call | tf_op jit(solution)/shard_map/pallas_call | solution.py:347
  128.4 3.3 %collective-permute-start.1 = (f32[640,128]{1,0:T(8,128)S(1)}, f32[640,128]{1,0:T(8,128)S(1)}, u32[]{:S(2)}, u32[]{:S(2)}) collective-permute-start(f32[640,128]{1,0:T(8,128)S(1)} %get-tuple-element.8), channel_id=1, source_target_pairs={{0,1},{1,0},{2,3},{3,2},{4,5},{5,4},{6,7},{7,6},{8,9},{9,8},{10,11... | collective-permute-start | bytes 983048 | tf_op jit(solution)/shard_map/ppermute | solution.py:422
  131.7 1.3 collective-permute-done.1
  133.0 11.5 %all_to_all.33 = f32[16,40,128]{2,1,0:T(8,128)S(1)} all-to-all(f32[16,40,128]{2,1,0:T(8,128)S(1)} %bitcast.15), channel_id=1, replica_groups={{0,2,4,6,8,10,12,14,16,18,20,22,24,26,28,30},{1,3,5,7,9,11,13,15,17,19,..., dimensions={0} | all-to-all | bytes 655360 | tf_op jit(solution)/shard_map/all_to_all | solution.py:407
  144.6 10.8 %all_to_all.34 = f32[8,40,128]{2,1,0:T(8,128)S(1)} all-to-all(f32[8,40,128]{2,1,0:T(8,128)S(1)} %broadcast_in_dim.10), channel_id=1, replica_groups=mesh['sp'=8,'gx'=32] {'sp'}, dimensions={0} | all-to-all | bytes 327680 | tf_op jit(solution)/shard_map/all_to_all | solution.py:424
  155.4 10.6 %all_to_all.35 = f32[16,40,128]{2,1,0:T(8,128)S(1)} all-to-all(f32[16,40,128]{2,1,0:T(8,128)S(1)} %broadcast_in_dim.11), channel_id=1, replica_groups={{0,2,4,6,8,10,12,14,16,18,20,22,24,26,28,30},{1,3,5,7,9,11,13,15,17,19,..., dimensions={0} | all-to-all | bytes 655360 | tf_op jit(solution)/shard_map/all_to_all | solution.py:407
  166.0 3.9 %collective-permute-start.2 = (f32[640,128]{1,0:T(8,128)S(1)}, f32[640,128]{1,0:T(8,128)S(1)}, u32[]{:S(2)}, u32[]{:S(2)}) collective-permute-start(f32[640,128]{1,0:T(8,128)S(1)} %bitcast.11), channel_id=1, source_target_pairs={{0,1},{1,0},{2,3},{3,2},{4,5},{5,4},{6,7},{7,6},{8,9},{9,8},{10,11... | collective-permute-start | bytes 983048 | tf_op jit(solution)/shard_map/ppermute | solution.py:426
  169.9 1.3 collective-permute-done.2.other_ref
  171.1 0.0 copy-done
  171.1 15.4 %shard_map.53 = (f32[384,128]{1,0:T(8,128)}, f32[16,24]{1,0:T(8,128)}) custom-call(f32[640,128]{1,0:T(8,128)S(1)} %bitcast.12, f32[640,128]{1,0:T(8,128)S(1)} %collective-permute-done.2.other_ref, f32[32768,512]{1,0:T(8,128)} %get-tuple-element.9.turned_hbm, f32[512,128]{1,0:T(8,128)S(1)} %copy-done), custom_call_target="tpu_custom_call" | custom-call | tf_op jit(solution)/shard_map/pallas_call | solution.py:397
  (9 shorter events, 0.2 us)
Async XLA Ops:
  94.8 26.3 %copy-start.1 = (f32[64,16]{0,1:T(8,128)S(1)}, f32[64,16]{0,1:T(8,128)}, u32[]{:S(2)}) copy-start(f32[64,16]{0,1:T(8,128)} %param.4) | copy-start | bytes 12292
  98.3 1.7 collective-permute-start
  121.1 50.0 %copy-start = (f32[512,128]{1,0:T(8,128)S(1)}, f32[512,128]{1,0:T(8,128)}, u32[]{:S(2)}) copy-start(f32[512,128]{1,0:T(8,128)} %start_ref.1) | copy-start | bytes 786436
  128.4 4.6 %collective-permute-start.1 = (f32[640,128]{1,0:T(8,128)S(1)}, f32[640,128]{1,0:T(8,128)S(1)}, u32[]{:S(2)}, u32[]{:S(2)}) collective-permute-start(f32[640,128]{1,0:T(8,128)S(1)} %get-tuple-element.8), channel_id=1, source_target_pairs={{0,1},{1,0},{2,3},{3,2},{4,5},{5,4},{6,7},{7,6},{8,9},{9,8},{10,11... | collective-permute-start | bytes 983048 | tf_op jit(solution)/shard_map/ppermute | solution.py:422
  166.0 5.2 %collective-permute-start.2 = (f32[640,128]{1,0:T(8,128)S(1)}, f32[640,128]{1,0:T(8,128)S(1)}, u32[]{:S(2)}, u32[]{:S(2)}) collective-permute-start(f32[640,128]{1,0:T(8,128)S(1)} %bitcast.11), channel_id=1, source_target_pairs={{0,1},{1,0},{2,3},{3,2},{4,5},{5,4},{6,7},{7,6},{8,9},{9,8},{10,11... | collective-permute-start | bytes 983048 | tf_op jit(solution)/shard_map/ppermute | solution.py:426

commit v4 on v3

--- a/solution.py
+++ b/solution.py
@@ -57,9 +57,9 @@
     high, mid, low = a
     left = jnp.concatenate([high, mid, low], axis=1)
     got = bf16_dot(left, jnp.concatenate([high, mid], axis=1), TN)
-    small = got[256:384, 0:128]
+    small = got[256:384, 0:128] + bf16_dot(high, low, TN)
     cross = got[0:128, 128:256] + got[128:256, 0:128]
-    return got[0:128, 0:128] + (cross + (got[128:256, 128:256] + (small + small.T)))
+    return got[0:128, 0:128] + (cross + (got[128:256, 128:256] + small))
 
 
 def across(x, j):
@@ -150,7 +150,7 @@
     return result
 
 
-def subspace(gram, start, image_ref):
+def subspace(gram, start, image_ref, aside):
     split_gram = split3(gram)
     image_block = six(split_gram, split3(start))
     chunk = gram.shape[0] // CHUNKS
@@ -160,6 +160,7 @@
         last = sweep + 1 == SWEEPS
 
         def ahead(panel):
+            aside(sweep, panel)
             if panel < CHUNKS and not last:
                 rows = slice(chunk * panel, chunk * (panel + 1))
                 image_ref[rows, :] = six(tuple(g[rows] for g in split_gram), pieces)
@@ -363,7 +364,7 @@
 
 
 def core_kernel(
-    mine_ref, other_ref, turned_hbm, start_ref, out_ref, peaks_ref, image_ref, turned_ref, sem
+    mine_ref, other_ref, turned_hbm, start_ref, out_ref, peaks_ref, image_ref, turned_ref, high_ref, low_ref, sem
 ):
     copy = pltpu.make_async_copy(turned_hbm.at[pl.ds(0, 512)], turned_ref, sem)
     copy.start()
@@ -381,11 +382,18 @@
     gram = jnp.concatenate(
         [jnp.concatenate([blocks[i, j] for j in range(4)], axis=1) for i in range(4)], axis=0
     )
-    basis = subspace(gram, start_ref[...], image_ref)
-    copy.wait()
-    th, tl = split2(turned_ref[...].T)
+
+    def aside(sweep, panel):
+        if sweep == 1 and panel < 4:
+            if panel == 0:
+                copy.wait()
+            lanes = slice(128 * panel, 128 * (panel + 1))
+            high_ref[:, lanes], low_ref[:, lanes] = split2(turned_ref[lanes, :].T)
+
+    basis = subspace(gram, start_ref[...], image_ref, aside)
     bh, bl = split2(basis)
-    core = bf16_dot(th, bh) + bf16_dot(th, bl) + bf16_dot(tl, bh)
+    wide = bf16_dot(high_ref[...], jnp.concatenate([bh, bl], axis=1))
+    core = wide[:, 0:128] + (wide[:, 128:256] + bf16_dot(low_ref[...], bh))
     for r in range(16):
         out_ref[pl.ds(r, 24, stride=16), :] = core[32 * r : 32 * r + 24, :]
     peaks = jnp.max(jnp.abs(core).reshape(16, 32, 128), axis=2)
@@ -398,7 +406,13 @@
         core_kernel,
         out_shape=(jax.ShapeDtypeStruct((384, 128), F32), jax.ShapeDtypeStruct((16, 24), F32)),
         in_specs=[whole, whole, pl.BlockSpec(memory_space=pltpu.HBM), whole],
-        scratch_shapes=[pltpu.VMEM((512, 128), F32), pltpu.VMEM((512, 512), F32), pltpu.SemaphoreType.DMA],
+        scratch_shapes=[
+            pltpu.VMEM((512, 128), F32),
+            pltpu.VMEM((512, 512), F32),
+            pltpu.VMEM((512, 512), BF16),
+            pltpu.VMEM((512, 512), BF16),
+            pltpu.SemaphoreType.DMA,
+        ],
         compiler_params=grant(20),
     )(mine, other, turned, start_plane)
 

time: 187 us -> 186 us (level)
  no operation moved by 1% of the time
where the time goes in v4:
time: 186 us
  blocking collectives  145 us (78%)
  Pallas kernels  28.2 us (15%)
  starting transfers between devices  8.11 us (4%)
  waiting for transfers between devices  3.35 us (2%)
    all_to_all x1, blocking collectives, per_device(): received = lax.all_to_all(sent, BOTH, 0, 0, tiled=True).reshape(8, 768, 128)  91.1 us
    all_to_all x3, blocking collectives, over_plane(): return lax.all_to_all(x, 'gx', 0, 0, tiled=True, axis_index_groups=PLANES)  32.5 us
    pallas_call x1, Pallas kernels, core_of(): pl.pallas_call(core_kernel, out_shape=(jax.ShapeDtypeStruct((384, 128), F...  14.6 us
    all_to_all x1, blocking collectives, per_device(): lax.all_to_all(copies(share, 8), 'sp', 0, 0, tiled=True)  10.8 us
    all_to_all x1, blocking collectives, per_device(): lax.all_to_all(copies(grams, 8), 'sp', 0, 0, tiled=True)  10.7 us
    pallas_call x1, Pallas kernels, plane_gram(): pl.pallas_call(plane_gram_kernel, out_shape=(jax.ShapeDtypeStruct((SPARE,...  7.08 us
    ppermute x1, starting transfers between devices, per_device(): other = lax.ppermute(mine, 'gx', PAIR)  3.9 us
  transfers between devices with their start and end apart: 3, of which 3 were waited for; matrix products, arithmetic and copies ran while one was open for 0% of the time, Pallas kernels for 0%

profile of v4, /device:TPU:1, one launch (start us, length us, event | category | flops | bytes accessed | tf_op | source)
XLA Modules:
  0.0 185.7 jit_solution(17056723824422280345)
XLA Ops:
  0.6 3.1 %shard_map.50 = f32[6144,128]{1,0:T(8,128)S(1)} custom-call(f32[128,6144]{1,0:T(8,128)} %bitcast.14), custom_call_target="tpu_custom_call" | custom-call | tf_op jit(solution)/shard_map/pallas_call | solution.py:208
  3.7 91.1 %all_to_all.30 = f32[256,24,128]{2,1,0:T(8,128)S(1)} all-to-all(f32[256,24,128]{2,1,0:T(8,128)S(1)} %bitcast.10), channel_id=1, replica_groups=mesh['sp'=8,'gx'=32] {'sp','gx'}, dimensions={0} | all-to-all | bytes 6291456 | tf_op jit(solution)/shard_map/all_to_all | solution.py:430
  94.8 0.0 copy-start.1
  94.8 3.5 %shard_map.51 = f32[24,128]{1,0:T(8,128)S(1)} custom-call(f32[8,768,128]{2,1,0:T(8,128)S(1)} %bitcast.8), custom_call_target="tpu_custom_call" | custom-call | tf_op jit(solution)/shard_map/pallas_call | solution.py:258
  98.3 0.9 collective-permute-start
  99.1 0.8 collective-permute-done
  100.0 10.7 %all_to_all.31 = f32[8,24,128]{2,1,0:T(8,128)S(1)} all-to-all(f32[8,24,128]{2,1,0:T(8,128)S(1)} %broadcast_in_dim.8), channel_id=1, replica_groups=mesh['sp'=8,'gx'=32] {'sp'}, dimensions={0} | all-to-all | bytes 196608 | tf_op jit(solution)/shard_map/all_to_all | solution.py:433
  110.7 10.4 %all_to_all.32.g_ref = f32[16,24,128]{2,1,0:T(8,128)S(1)} all-to-all(f32[16,24,128]{2,1,0:T(8,128)S(1)} %broadcast_in_dim.9), channel_id=1, replica_groups={{0,2,4,6,8,10,12,14,16,18,20,22,24,26,28,30},{1,3,5,7,9,11,13,15,17,19,..., dimensions={0} | all-to-all | bytes 393216 | tf_op jit(solution)/shard_map/all_to_all | solution.py:421
  121.1 0.0 copy-done.1
  121.1 0.0 copy-start
  121.1 7.1 %shard_map.52 = (f32[32768,512]{1,0:T(8,128)}, f32[640,128]{1,0:T(8,128)S(1)}, f32[640,128]{1,0:T(8,128)S(1)}) custom-call(f32[8,768,128]{2,1,0:T(8,128)S(1)} %bitcast.9, f32[16,24,128]{2,1,0:T(8,128)S(1)} %all_to_all.32.g_ref, f32[16,64]{1,0:T(8,128)S(1)} %bitcast.13), custom_call_target="tpu_custom_call" | custom-call | tf_op jit(solution)/shard_map/pallas_call | solution.py:348
  128.2 3.3 %collective-permute-start.1 = (f32[640,128]{1,0:T(8,128)S(1)}, f32[640,128]{1,0:T(8,128)S(1)}, u32[]{:S(2)}, u32[]{:S(2)}) collective-permute-start(f32[640,128]{1,0:T(8,128)S(1)} %get-tuple-element.8), channel_id=1, source_target_pairs={{0,1},{1,0},{2,3},{3,2},{4,5},{5,4},{6,7},{7,6},{8,9},{9,8},{10,11... | collective-permute-start | bytes 983048 | tf_op jit(solution)/shard_map/ppermute | solution.py:436
  131.5 1.3 collective-permute-done.1
  132.8 11.5 %all_to_all.33 = f32[16,40,128]{2,1,0:T(8,128)S(1)} all-to-all(f32[16,40,128]{2,1,0:T(8,128)S(1)} %bitcast.15), channel_id=1, replica_groups={{0,2,4,6,8,10,12,14,16,18,20,22,24,26,28,30},{1,3,5,7,9,11,13,15,17,19,..., dimensions={0} | all-to-all | bytes 655360 | tf_op jit(solution)/shard_map/all_to_all | solution.py:421
  144.4 10.8 %all_to_all.34 = f32[8,40,128]{2,1,0:T(8,128)S(1)} all-to-all(f32[8,40,128]{2,1,0:T(8,128)S(1)} %broadcast_in_dim.10), channel_id=1, replica_groups=mesh['sp'=8,'gx'=32] {'sp'}, dimensions={0} | all-to-all | bytes 327680 | tf_op jit(solution)/shard_map/all_to_all | solution.py:438
  155.2 10.6 %all_to_all.35 = f32[16,40,128]{2,1,0:T(8,128)S(1)} all-to-all(f32[16,40,128]{2,1,0:T(8,128)S(1)} %broadcast_in_dim.11), channel_id=1, replica_groups={{0,2,4,6,8,10,12,14,16,18,20,22,24,26,28,30},{1,3,5,7,9,11,13,15,17,19,..., dimensions={0} | all-to-all | bytes 655360 | tf_op jit(solution)/shard_map/all_to_all | solution.py:421
  165.8 3.9 %collective-permute-start.2 = (f32[640,128]{1,0:T(8,128)S(1)}, f32[640,128]{1,0:T(8,128)S(1)}, u32[]{:S(2)}, u32[]{:S(2)}) collective-permute-start(f32[640,128]{1,0:T(8,128)S(1)} %bitcast.11), channel_id=1, source_target_pairs={{0,1},{1,0},{2,3},{3,2},{4,5},{5,4},{6,7},{7,6},{8,9},{9,8},{10,11... | collective-permute-start | bytes 983048 | tf_op jit(solution)/shard_map/ppermute | solution.py:440
  169.7 1.3 collective-permute-done.2.other_ref
  170.9 0.0 copy-done
  170.9 14.6 %shard_map.53 = (f32[384,128]{1,0:T(8,128)}, f32[16,24]{1,0:T(8,128)}) custom-call(f32[640,128]{1,0:T(8,128)S(1)} %bitcast.12, f32[640,128]{1,0:T(8,128)S(1)} %collective-permute-done.2.other_ref, f32[32768,512]{1,0:T(8,128)} %get-tuple-element.9.turned_hbm, f32[512,128]{1,0:T(8,128)S(1)} %copy-done), custom_call_target="tpu_custom_call" | custom-call | tf_op jit(solution)/shard_map/pallas_call | solution.py:405
  (9 shorter events, 0.2 us)
Async XLA Ops:
  94.8 26.3 %copy-start.1 = (f32[64,16]{0,1:T(8,128)S(1)}, f32[64,16]{0,1:T(8,128)}, u32[]{:S(2)}) copy-start(f32[64,16]{0,1:T(8,128)} %param.4) | copy-start | bytes 12292
  98.3 1.7 collective-permute-start
  121.1 49.9 %copy-start = (f32[512,128]{1,0:T(8,128)S(1)}, f32[512,128]{1,0:T(8,128)}, u32[]{:S(2)}) copy-start(f32[512,128]{1,0:T(8,128)} %start_ref.1) | copy-start | bytes 786436
  128.2 4.6 %collective-permute-start.1 = (f32[640,128]{1,0:T(8,128)S(1)}, f32[640,128]{1,0:T(8,128)S(1)}, u32[]{:S(2)}, u32[]{:S(2)}) collective-permute-start(f32[640,128]{1,0:T(8,128)S(1)} %get-tuple-element.8), channel_id=1, source_target_pairs={{0,1},{1,0},{2,3},{3,2},{4,5},{5,4},{6,7},{7,6},{8,9},{9,8},{10,11... | collective-permute-start | bytes 983048 | tf_op jit(solution)/shard_map/ppermute | solution.py:436
  165.8 5.2 %collective-permute-start.2 = (f32[640,128]{1,0:T(8,128)S(1)}, f32[640,128]{1,0:T(8,128)S(1)}, u32[]{:S(2)}, u32[]{:S(2)}) collective-permute-start(f32[640,128]{1,0:T(8,128)S(1)} %bitcast.11), channel_id=1, source_target_pairs={{0,1},{1,0},{2,3},{3,2},{4,5},{5,4},{6,7},{7,6},{8,9},{9,8},{10,11... | collective-permute-start | bytes 983048 | tf_op jit(solution)/shard_map/ppermute | solution.py:440

commit v5 on v4

--- a/solution.py
+++ b/solution.py
@@ -299,9 +299,11 @@
         high, low = split2(weights)
         wh_ref[128 * s : 128 * (s + 1), :] = high
         wl_ref[128 * s : 128 * (s + 1), :] = low
-    wh = wh_ref[...]
-    total = bf16_dot(h_ref[...], wh) + (bf16_dot(h_ref[...], wl_ref[...]) + bf16_dot(l_ref[...], wh))
-    red_ref[...] = total
+    wh, wl = wh_ref[...], wl_ref[...]
+    for n in range(2):
+        rows = slice(384 * n, 384 * (n + 1))
+        high = h_ref[rows, :]
+        red_ref[rows, :] = bf16_dot(high, wh) + (bf16_dot(high, wl) + bf16_dot(l_ref[rows, :], wh))
     lane = lax.broadcasted_iota(jnp.int32, (24, 128), 1)
     blank = jnp.zeros((8, 128), F32)
     for pair in range(16):

time: 186 us -> 185 us (level)
  no operation moved by 1% of the time
where the time goes in v5:
time: 185 us
  blocking collectives  145 us (78%)
  Pallas kernels  27.6 us (15%)
  starting transfers between devices  7.93 us (4%)
  waiting for transfers between devices  3.35 us (2%)
    all_to_all x1, blocking collectives, per_device(): received = lax.all_to_all(sent, BOTH, 0, 0, tiled=True).reshape(8, 768, 128)  91.1 us
    all_to_all x3, blocking collectives, over_plane(): return lax.all_to_all(x, 'gx', 0, 0, tiled=True, axis_index_groups=PLANES)  32.5 us
    pallas_call x1, Pallas kernels, core_of(): pl.pallas_call(core_kernel, out_shape=(jax.ShapeDtypeStruct((384, 128), F...  14.6 us
    all_to_all x1, blocking collectives, per_device(): lax.all_to_all(copies(share, 8), 'sp', 0, 0, tiled=True)  10.8 us
    all_to_all x1, blocking collectives, per_device(): lax.all_to_all(copies(grams, 8), 'sp', 0, 0, tiled=True)  10.7 us
    pallas_call x1, Pallas kernels, plane_gram(): pl.pallas_call(plane_gram_kernel, out_shape=(jax.ShapeDtypeStruct((SPARE,...  6.44 us
    ppermute x1, starting transfers between devices, per_device(): other = lax.ppermute(mine, 'gx', PAIR)  3.9 us
  transfers between devices with their start and end apart: 3, of which 3 were waited for; matrix products, arithmetic and copies ran while one was open for 0% of the time, Pallas kernels for 0%

profile of v5, /device:TPU:1, one launch (start us, length us, event | category | flops | bytes accessed | tf_op | source)
XLA Modules:
  0.0 184.9 jit_solution(11064886871175623206)
XLA Ops:
  0.6 3.1 %shard_map.50 = f32[6144,128]{1,0:T(8,128)S(1)} custom-call(f32[128,6144]{1,0:T(8,128)} %bitcast.14), custom_call_target="tpu_custom_call" | custom-call | tf_op jit(solution)/shard_map/pallas_call | solution.py:208
  3.7 91.1 %all_to_all.30 = f32[256,24,128]{2,1,0:T(8,128)S(1)} all-to-all(f32[256,24,128]{2,1,0:T(8,128)S(1)} %bitcast.10), channel_id=1, replica_groups=mesh['sp'=8,'gx'=32] {'sp','gx'}, dimensions={0} | all-to-all | bytes 6291456 | tf_op jit(solution)/shard_map/all_to_all | solution.py:432
  94.8 0.0 copy-start.1
  94.8 3.5 %shard_map.51 = f32[24,128]{1,0:T(8,128)S(1)} custom-call(f32[8,768,128]{2,1,0:T(8,128)S(1)} %bitcast.8), custom_call_target="tpu_custom_call" | custom-call | tf_op jit(solution)/shard_map/pallas_call | solution.py:258
  98.3 0.9 collective-permute-start
  99.1 0.8 collective-permute-done
  100.0 10.7 %all_to_all.31 = f32[8,24,128]{2,1,0:T(8,128)S(1)} all-to-all(f32[8,24,128]{2,1,0:T(8,128)S(1)} %broadcast_in_dim.8), channel_id=1, replica_groups=mesh['sp'=8,'gx'=32] {'sp'}, dimensions={0} | all-to-all | bytes 196608 | tf_op jit(solution)/shard_map/all_to_all | solution.py:435
  110.7 10.4 %all_to_all.32.g_ref = f32[16,24,128]{2,1,0:T(8,128)S(1)} all-to-all(f32[16,24,128]{2,1,0:T(8,128)S(1)} %broadcast_in_dim.9), channel_id=1, replica_groups={{0,2,4,6,8,10,12,14,16,18,20,22,24,26,28,30},{1,3,5,7,9,11,13,15,17,19,..., dimensions={0} | all-to-all | bytes 393216 | tf_op jit(solution)/shard_map/all_to_all | solution.py:423
  121.1 0.0 copy-done.1
  121.1 0.0 copy-start
  121.1 6.4 %shard_map.52 = (f32[32768,512]{1,0:T(8,128)}, f32[640,128]{1,0:T(8,128)S(1)}, f32[640,128]{1,0:T(8,128)S(1)}) custom-call(f32[8,768,128]{2,1,0:T(8,128)S(1)} %bitcast.9, f32[16,24,128]{2,1,0:T(8,128)S(1)} %all_to_all.32.g_ref, f32[16,64]{1,0:T(8,128)S(1)} %bitcast.13), custom_call_target="tpu_custom_call" | custom-call | tf_op jit(solution)/shard_map/pallas_call | solution.py:350
  127.5 3.2 %collective-permute-start.1 = (f32[640,128]{1,0:T(8,128)S(1)}, f32[640,128]{1,0:T(8,128)S(1)}, u32[]{:S(2)}, u32[]{:S(2)}) collective-permute-start(f32[640,128]{1,0:T(8,128)S(1)} %get-tuple-element.8), channel_id=1, source_target_pairs={{0,1},{1,0},{2,3},{3,2},{4,5},{5,4},{6,7},{7,6},{8,9},{9,8},{10,11... | collective-permute-start | bytes 983048 | tf_op jit(solution)/shard_map/ppermute | solution.py:438
  130.7 1.3 collective-permute-done.1
  132.0 11.5 %all_to_all.33 = f32[16,40,128]{2,1,0:T(8,128)S(1)} all-to-all(f32[16,40,128]{2,1,0:T(8,128)S(1)} %bitcast.15), channel_id=1, replica_groups={{0,2,4,6,8,10,12,14,16,18,20,22,24,26,28,30},{1,3,5,7,9,11,13,15,17,19,..., dimensions={0} | all-to-all | bytes 655360 | tf_op jit(solution)/shard_map/all_to_all | solution.py:423
  143.6 10.8 %all_to_all.34 = f32[8,40,128]{2,1,0:T(8,128)S(1)} all-to-all(f32[8,40,128]{2,1,0:T(8,128)S(1)} %broadcast_in_dim.10), channel_id=1, replica_groups=mesh['sp'=8,'gx'=32] {'sp'}, dimensions={0} | all-to-all | bytes 327680 | tf_op jit(solution)/shard_map/all_to_all | solution.py:440
  154.4 10.6 %all_to_all.35 = f32[16,40,128]{2,1,0:T(8,128)S(1)} all-to-all(f32[16,40,128]{2,1,0:T(8,128)S(1)} %broadcast_in_dim.11), channel_id=1, replica_groups={{0,2,4,6,8,10,12,14,16,18,20,22,24,26,28,30},{1,3,5,7,9,11,13,15,17,19,..., dimensions={0} | all-to-all | bytes 655360 | tf_op jit(solution)/shard_map/all_to_all | solution.py:423
  165.0 3.9 %collective-permute-start.2 = (f32[640,128]{1,0:T(8,128)S(1)}, f32[640,128]{1,0:T(8,128)S(1)}, u32[]{:S(2)}, u32[]{:S(2)}) collective-permute-start(f32[640,128]{1,0:T(8,128)S(1)} %bitcast.11), channel_id=1, source_target_pairs={{0,1},{1,0},{2,3},{3,2},{4,5},{5,4},{6,7},{7,6},{8,9},{9,8},{10,11... | collective-permute-start | bytes 983048 | tf_op jit(solution)/shard_map/ppermute | solution.py:442
  168.9 1.3 collective-permute-done.2.other_ref
  170.1 0.0 copy-done
  170.1 14.6 %shard_map.53 = (f32[384,128]{1,0:T(8,128)}, f32[16,24]{1,0:T(8,128)}) custom-call(f32[640,128]{1,0:T(8,128)S(1)} %bitcast.12, f32[640,128]{1,0:T(8,128)S(1)} %collective-permute-done.2.other_ref, f32[32768,512]{1,0:T(8,128)} %get-tuple-element.9.turned_hbm, f32[512,128]{1,0:T(8,128)S(1)} %copy-done), custom_call_target="tpu_custom_call" | custom-call | tf_op jit(solution)/shard_map/pallas_call | solution.py:407
  (9 shorter events, 0.2 us)
Async XLA Ops:
  94.8 26.3 %copy-start.1 = (f32[64,16]{0,1:T(8,128)S(1)}, f32[64,16]{0,1:T(8,128)}, u32[]{:S(2)}) copy-start(f32[64,16]{0,1:T(8,128)} %param.4) | copy-start | bytes 12292
  98.3 1.7 collective-permute-start
  121.1 49.0 %copy-start = (f32[512,128]{1,0:T(8,128)S(1)}, f32[512,128]{1,0:T(8,128)}, u32[]{:S(2)}) copy-start(f32[512,128]{1,0:T(8,128)} %start_ref.1) | copy-start | bytes 786436
  127.5 4.4 %collective-permute-start.1 = (f32[640,128]{1,0:T(8,128)S(1)}, f32[640,128]{1,0:T(8,128)S(1)}, u32[]{:S(2)}, u32[]{:S(2)}) collective-permute-start(f32[640,128]{1,0:T(8,128)S(1)} %get-tuple-element.8), channel_id=1, source_target_pairs={{0,1},{1,0},{2,3},{3,2},{4,5},{5,4},{6,7},{7,6},{8,9},{9,8},{10,11... | collective-permute-start | bytes 983048 | tf_op jit(solution)/shard_map/ppermute | solution.py:438
  165.0 5.2 %collective-permute-start.2 = (f32[640,128]{1,0:T(8,128)S(1)}, f32[640,128]{1,0:T(8,128)S(1)}, u32[]{:S(2)}, u32[]{:S(2)}) collective-permute-start(f32[640,128]{1,0:T(8,128)S(1)} %bitcast.11), channel_id=1, source_target_pairs={{0,1},{1,0},{2,3},{3,2},{4,5},{5,4},{6,7},{7,6},{8,9},{9,8},{10,11... | collective-permute-start | bytes 983048 | tf_op jit(solution)/shard_map/ppermute | solution.py:442

commit v6 on v5

--- a/solution.py
+++ b/solution.py
@@ -396,8 +396,8 @@
     bh, bl = split2(basis)
     wide = bf16_dot(high_ref[...], jnp.concatenate([bh, bl], axis=1))
     core = wide[:, 0:128] + (wide[:, 128:256] + bf16_dot(low_ref[...], bh))
-    for r in range(16):
-        out_ref[pl.ds(r, 24, stride=16), :] = core[32 * r : 32 * r + 24, :]
+    ranks = jnp.concatenate([core[32 * r : 32 * r + 24, :].reshape(1, 24, 128) for r in range(16)], axis=0)
+    out_ref[...] = jnp.swapaxes(ranks, 0, 1)
     peaks = jnp.max(jnp.abs(core).reshape(16, 32, 128), axis=2)
     peaks_ref[...] = peaks[:, 0:24]
 
@@ -406,7 +406,7 @@
     whole = pl.BlockSpec(memory_space=pltpu.VMEM)
     return pl.pallas_call(
         core_kernel,
-        out_shape=(jax.ShapeDtypeStruct((384, 128), F32), jax.ShapeDtypeStruct((16, 24), F32)),
+        out_shape=(jax.ShapeDtypeStruct((24, 16, 128), F32), jax.ShapeDtypeStruct((16, 24), F32)),
         in_specs=[whole, whole, pl.BlockSpec(memory_space=pltpu.HBM), whole],
         scratch_shapes=[
             pltpu.VMEM((512, 128), F32),
@@ -441,7 +441,7 @@
     mine = over_plane(copies(share, 16)).reshape(640, 128)
     other = lax.ppermute(mine, "gx", PAIR)
     core_block, block_peaks = core_of(mine, other, turned, start_plane)
-    return core_block.reshape(24, 16, 128), block_peaks.T
+    return core_block, block_peaks.T
 
 
 def solution(mesh):

time: 185 us -> 185 us (level)
  no operation moved by 1% of the time
where the time goes in v6:
time: 185 us
  blocking collectives  145 us (78%)
  Pallas kernels  27.6 us (15%)
  starting transfers between devices  7.93 us (4%)
  waiting for transfers between devices  3.35 us (2%)
    all_to_all x1, blocking collectives, per_device(): received = lax.all_to_all(sent, BOTH, 0, 0, tiled=True).reshape(8, 768, 128)  91.1 us
    all_to_all x3, blocking collectives, over_plane(): return lax.all_to_all(x, 'gx', 0, 0, tiled=True, axis_index_groups=PLANES)  32.5 us
    pallas_call x1, Pallas kernels, core_of(): pl.pallas_call(core_kernel, out_shape=(jax.ShapeDtypeStruct((24, 16, 128)...  14.6 us
    all_to_all x1, blocking collectives, per_device(): lax.all_to_all(copies(share, 8), 'sp', 0, 0, tiled=True)  10.8 us
    all_to_all x1, blocking collectives, per_device(): lax.all_to_all(copies(grams, 8), 'sp', 0, 0, tiled=True)  10.7 us
    pallas_call x1, Pallas kernels, plane_gram(): pl.pallas_call(plane_gram_kernel, out_shape=(jax.ShapeDtypeStruct((SPARE,...  6.44 us
    ppermute x1, starting transfers between devices, per_device(): other = lax.ppermute(mine, 'gx', PAIR)  3.9 us
  transfers between devices with their start and end apart: 3, of which 3 were waited for; matrix products, arithmetic and copies ran while one was open for 0% of the time, Pallas kernels for 0%

profile of v6, /device:TPU:1, one launch (start us, length us, event | category | flops | bytes accessed | tf_op | source)
XLA Modules:
  0.0 184.9 jit_solution(11554516240684648860)
XLA Ops:
  0.6 3.1 %shard_map.50 = f32[6144,128]{1,0:T(8,128)S(1)} custom-call(f32[128,6144]{1,0:T(8,128)} %bitcast.13), custom_call_target="tpu_custom_call" | custom-call | tf_op jit(solution)/shard_map/pallas_call | solution.py:208
  3.7 91.1 %all_to_all.30 = f32[256,24,128]{2,1,0:T(8,128)S(1)} all-to-all(f32[256,24,128]{2,1,0:T(8,128)S(1)} %bitcast.9), channel_id=1, replica_groups=mesh['sp'=8,'gx'=32] {'sp','gx'}, dimensions={0} | all-to-all | bytes 6291456 | tf_op jit(solution)/shard_map/all_to_all | solution.py:432
  94.8 0.0 copy-start.1
  94.8 3.5 %shard_map.51 = f32[24,128]{1,0:T(8,128)S(1)} custom-call(f32[8,768,128]{2,1,0:T(8,128)S(1)} %bitcast.7), custom_call_target="tpu_custom_call" | custom-call | tf_op jit(solution)/shard_map/pallas_call | solution.py:258
  98.3 0.9 collective-permute-start
  99.1 0.8 collective-permute-done
  100.0 10.7 %all_to_all.31 = f32[8,24,128]{2,1,0:T(8,128)S(1)} all-to-all(f32[8,24,128]{2,1,0:T(8,128)S(1)} %broadcast_in_dim.8), channel_id=1, replica_groups=mesh['sp'=8,'gx'=32] {'sp'}, dimensions={0} | all-to-all | bytes 196608 | tf_op jit(solution)/shard_map/all_to_all | solution.py:435
  110.7 10.4 %all_to_all.32.g_ref = f32[16,24,128]{2,1,0:T(8,128)S(1)} all-to-all(f32[16,24,128]{2,1,0:T(8,128)S(1)} %broadcast_in_dim.9), channel_id=1, replica_groups={{0,2,4,6,8,10,12,14,16,18,20,22,24,26,28,30},{1,3,5,7,9,11,13,15,17,19,..., dimensions={0} | all-to-all | bytes 393216 | tf_op jit(solution)/shard_map/all_to_all | solution.py:423
  121.1 0.0 copy-done.1
  121.1 0.0 copy-start
  121.1 6.4 %shard_map.52 = (f32[32768,512]{1,0:T(8,128)}, f32[640,128]{1,0:T(8,128)S(1)}, f32[640,128]{1,0:T(8,128)S(1)}) custom-call(f32[8,768,128]{2,1,0:T(8,128)S(1)} %bitcast.8, f32[16,24,128]{2,1,0:T(8,128)S(1)} %all_to_all.32.g_ref, f32[16,64]{1,0:T(8,128)S(1)} %bitcast.12), custom_call_target="tpu_custom_call" | custom-call | tf_op jit(solution)/shard_map/pallas_call | solution.py:350
  127.5 3.2 %collective-permute-start.1 = (f32[640,128]{1,0:T(8,128)S(1)}, f32[640,128]{1,0:T(8,128)S(1)}, u32[]{:S(2)}, u32[]{:S(2)}) collective-permute-start(f32[640,128]{1,0:T(8,128)S(1)} %get-tuple-element.8), channel_id=1, source_target_pairs={{0,1},{1,0},{2,3},{3,2},{4,5},{5,4},{6,7},{7,6},{8,9},{9,8},{10,11... | collective-permute-start | bytes 983048 | tf_op jit(solution)/shard_map/ppermute | solution.py:438
  130.7 1.3 collective-permute-done.1
  132.0 11.5 %all_to_all.33 = f32[16,40,128]{2,1,0:T(8,128)S(1)} all-to-all(f32[16,40,128]{2,1,0:T(8,128)S(1)} %bitcast.14), channel_id=1, replica_groups={{0,2,4,6,8,10,12,14,16,18,20,22,24,26,28,30},{1,3,5,7,9,11,13,15,17,19,..., dimensions={0} | all-to-all | bytes 655360 | tf_op jit(solution)/shard_map/all_to_all | solution.py:423
  143.6 10.8 %all_to_all.34 = f32[8,40,128]{2,1,0:T(8,128)S(1)} all-to-all(f32[8,40,128]{2,1,0:T(8,128)S(1)} %broadcast_in_dim.10), channel_id=1, replica_groups=mesh['sp'=8,'gx'=32] {'sp'}, dimensions={0} | all-to-all | bytes 327680 | tf_op jit(solution)/shard_map/all_to_all | solution.py:440
  154.4 10.6 %all_to_all.35 = f32[16,40,128]{2,1,0:T(8,128)S(1)} all-to-all(f32[16,40,128]{2,1,0:T(8,128)S(1)} %broadcast_in_dim.11), channel_id=1, replica_groups={{0,2,4,6,8,10,12,14,16,18,20,22,24,26,28,30},{1,3,5,7,9,11,13,15,17,19,..., dimensions={0} | all-to-all | bytes 655360 | tf_op jit(solution)/shard_map/all_to_all | solution.py:423
  165.0 3.9 %collective-permute-start.2 = (f32[640,128]{1,0:T(8,128)S(1)}, f32[640,128]{1,0:T(8,128)S(1)}, u32[]{:S(2)}, u32[]{:S(2)}) collective-permute-start(f32[640,128]{1,0:T(8,128)S(1)} %bitcast.10), channel_id=1, source_target_pairs={{0,1},{1,0},{2,3},{3,2},{4,5},{5,4},{6,7},{7,6},{8,9},{9,8},{10,11... | collective-permute-start | bytes 983048 | tf_op jit(solution)/shard_map/ppermute | solution.py:442
  168.9 1.3 collective-permute-done.2.other_ref
  170.1 0.0 copy-done
  170.1 14.6 %shard_map.53 = (f32[24,16,128]{2,1,0:T(8,128)}, f32[16,24]{1,0:T(8,128)}) custom-call(f32[640,128]{1,0:T(8,128)S(1)} %bitcast.11, f32[640,128]{1,0:T(8,128)S(1)} %collective-permute-done.2.other_ref, f32[32768,512]{1,0:T(8,128)} %get-tuple-element.9.turned_hbm, f32[512,128]{1,0:T(8,128)S(1)} %copy-done), custom_call_target="tpu_custom_call" | custom-call | tf_op jit(solution)/shard_map/pallas_call | solution.py:407
  (9 shorter events, 0.2 us)
Async XLA Ops:
  94.8 26.3 %copy-start.1 = (f32[64,16]{0,1:T(8,128)S(1)}, f32[64,16]{0,1:T(8,128)}, u32[]{:S(2)}) copy-start(f32[64,16]{0,1:T(8,128)} %param.4) | copy-start | bytes 12292
  98.3 1.7 collective-permute-start
  121.1 49.0 %copy-start = (f32[512,128]{1,0:T(8,128)S(1)}, f32[512,128]{1,0:T(8,128)}, u32[]{:S(2)}) copy-start(f32[512,128]{1,0:T(8,128)} %start_ref.1) | copy-start | bytes 786436
  127.5 4.4 %collective-permute-start.1 = (f32[640,128]{1,0:T(8,128)S(1)}, f32[640,128]{1,0:T(8,128)S(1)}, u32[]{:S(2)}, u32[]{:S(2)}) collective-permute-start(f32[640,128]{1,0:T(8,128)S(1)} %get-tuple-element.8), channel_id=1, source_target_pairs={{0,1},{1,0},{2,3},{3,2},{4,5},{5,4},{6,7},{7,6},{8,9},{9,8},{10,11... | collective-permute-start | bytes 983048 | tf_op jit(solution)/shard_map/ppermute | solution.py:438
  165.0 5.2 %collective-permute-start.2 = (f32[640,128]{1,0:T(8,128)S(1)}, f32[640,128]{1,0:T(8,128)S(1)}, u32[]{:S(2)}, u32[]{:S(2)}) collective-permute-start(f32[640,128]{1,0:T(8,128)S(1)} %bitcast.10), channel_id=1, source_target_pairs={{0,1},{1,0},{2,3},{3,2},{4,5},{5,4},{6,7},{7,6},{8,9},{9,8},{10,11... | collective-permute-start | bytes 983048 | tf_op jit(solution)/shard_map/ppermute | solution.py:442
